TPU v7x, 512 devices: a whole 4x4x16 slice. The times are simulated.
512 devices in a mesh: tile: 64 (over z, y_lo, core), scan: 8 (over y_hi, x).
Axes of the slice: x: 4, y: 4 (y_hi: 2, y_lo: 2; y = y_hi * 2 + y_lo), z: 16, core: 2. Of those that a mesh axis runs over, the one named last changes fastest.
Arguments:
- object_slices: float32 [2, 4, 4096, 256], P(None, None, ('tile', 'scan')), may hold values from -1 to 1
- probe_wave: float32 [2, 128, 128], replicated, may hold values from -2.5 to 2.5
- offsets: int32 [1024, 2], P(('tile', 'scan')), may hold values from 0 to 128, as said below
- counts: int32 [512], P(('tile', 'scan')), may hold values from 0 to 2, as said below
- measured: float32 [1024, 128, 128], P(('tile', 'scan')), may hold values from 0.05 to 2
Outputs:
- updated_slices: float32 [2, 4, 4096, 256], P(None, None, ('tile', 'scan'))
Inputs may be any that keep to these rules, and one draw needn't show every extreme that they name: Slot p's patch starts at row (t * 64 - 128 / 2 + offsets[p, 0]) mod 4096, t the tile index holding slot p, and at column offsets[p, 1]; offsets[p, 0] < 64 and offsets[p, 1] <= 128. The counts of the devices of one tile index sum to 8 and one of them is 2; a device's slots at or past its count hold no position.
All inputs are finite; a program needn't handle non-finite values.
Results may differ from a plain program's by a relative error of at most 0.0003.
Values sent between devices are 32-bit elements; how exact they have to be, the bound alone decides.
A program may use at most 64 MiB of HBM per device.

v0:
```python
import math

import jax
import jax.numpy as jnp
from jax import lax
from jax.sharding import PartitionSpec as P

ITERS = 2


floor_power = 0.04
step_gain = 0.5
highest = lax.Precision.HIGHEST


def extended_2(value, sides, width):
    for axis, dim in sides:
        peers, length = (lax.axis_size(axis), value.shape[dim])
        up = [(i, (i + 1) % peers) for i in range(peers)]
        down = [(j, i) for i, j in up]
        last = lax.slice_in_dim(value, length - width, length, axis=dim)
        first = lax.slice_in_dim(value, 0, width, axis=dim)
        before = lax.ppermute(last, axis, up)
        after = lax.ppermute(first, axis, down)
        value = jnp.concatenate([before, value, after], axis=dim)
    return value


def matmul_high(first, second):
    return jnp.dot(first, second, precision=highest, preferred_element_type=jnp.float32)


def operators(side):
    indices = jnp.arange(side, dtype=jnp.int32)
    phases = indices[:, None] * indices[None, :] % side
    angles = phases.astype(jnp.float32) * (2.0 * math.pi / side)
    norm_scale = 1.0 / math.sqrt(side)
    dft_re = jnp.cos(angles) * norm_scale
    dft_im = -jnp.sin(angles) * norm_scale
    frequency = (indices + side // 2) % side - side // 2
    kernel_angles = -math.pi / (2.0 * side) * (frequency * frequency).astype(jnp.float32)
    kernel_re = jnp.cos(kernel_angles)
    kernel_im = jnp.sin(kernel_angles)
    scaled_re = kernel_re[:, None] * dft_re - kernel_im[:, None] * dft_im
    scaled_im = kernel_re[:, None] * dft_im + kernel_im[:, None] * dft_re
    prop_re = matmul_high(dft_re, scaled_re) + matmul_high(dft_im, scaled_im)
    prop_im = matmul_high(dft_re, scaled_im) - matmul_high(dft_im, scaled_re)
    return (dft_re, dft_im, prop_re, prop_im)


def apply_left(matrix, field):
    return jnp.einsum(
        "ij,pjk->pik", matrix, field, precision=highest, preferred_element_type=jnp.float32
    )


def apply_right(field, matrix):
    return jnp.einsum(
        "pik,lk->pil", field, matrix, precision=highest, preferred_element_type=jnp.float32
    )


def sandwich(part_re, part_im, matrix_re, matrix_im):
    mid_re = apply_left(matrix_re, part_re) - apply_left(matrix_im, part_im)
    mid_im = apply_left(matrix_re, part_im) + apply_left(matrix_im, part_re)
    out_re = apply_right(mid_re, matrix_re) - apply_right(mid_im, matrix_im)
    out_im = apply_right(mid_re, matrix_im) + apply_right(mid_im, matrix_re)
    return (out_re, out_im)


def position_gradients(extended, probe_wave, offsets, measured, live_mask):
    side = probe_wave.shape[-1]
    slices = extended.shape[1]
    slot_total = offsets.shape[0]
    dft_re, dft_im, prop_re, prop_im = operators(side)
    adjoint_re = prop_re.T
    adjoint_im = -prop_im.T
    row_starts = offsets[:, 0]
    col_starts = offsets[:, 1]

    def cutter(plane):

        def cut(row_start, col_start):
            return lax.dynamic_slice(plane, (0, row_start, col_start), (slices, side, side))

        return jax.vmap(cut)(row_starts, col_starts)

    patch_re = cutter(extended[0])
    patch_im = cutter(extended[1])
    probe_re = probe_wave[0]
    probe_im = probe_wave[1]
    wave_re = probe_re * patch_re[:, 0] - probe_im * patch_im[:, 0]
    wave_im = probe_re * patch_im[:, 0] + probe_im * patch_re[:, 0]
    arrivals = [None] * slices
    for slice_index in range(1, slices):
        arrived_re, arrived_im = sandwich(wave_re, wave_im, prop_re, prop_im)
        arrivals[slice_index] = (arrived_re, arrived_im)
        wave_re = arrived_re * patch_re[:, slice_index] - arrived_im * patch_im[:, slice_index]
        wave_im = arrived_re * patch_im[:, slice_index] + arrived_im * patch_re[:, slice_index]
    far_re, far_im = sandwich(wave_re, wave_im, dft_re, dft_im)
    intensity = far_re * far_re + far_im * far_im
    amp_ratio = measured * lax.rsqrt(jnp.maximum(intensity, floor_power))
    live_gate = live_mask[:, None, None]
    chi_re = live_gate * (far_re - amp_ratio * far_re)
    chi_im = live_gate * (far_im - amp_ratio * far_im)
    back_re, back_im = sandwich(chi_re, chi_im, dft_re, -dft_im)
    grads_re = [None] * slices
    grads_im = [None] * slices
    for slice_index in range(slices - 1, 0, -1):
        in_re, in_im = arrivals[slice_index]
        grads_re[slice_index] = in_re * back_re + in_im * back_im
        grads_im[slice_index] = in_re * back_im - in_im * back_re
        turned_re = patch_re[:, slice_index] * back_re + patch_im[:, slice_index] * back_im
        turned_im = patch_re[:, slice_index] * back_im - patch_im[:, slice_index] * back_re
        back_re, back_im = sandwich(turned_re, turned_im, adjoint_re, adjoint_im)
    grads_re[0] = probe_re * back_re + probe_im * back_im
    grads_im[0] = probe_re * back_im - probe_im * back_re
    stacked_re = jnp.stack(grads_re, axis=1)
    stacked_im = jnp.stack(grads_im, axis=1)
    start_total = jnp.zeros((2,) + extended.shape[1:], jnp.float32)

    def add_one(position, running):
        row_start = row_starts[position]
        col_start = col_starts[position]
        for part_index, stacked in ((0, stacked_re), (1, stacked_im)):
            corner = (part_index, 0, row_start, col_start)
            present = lax.dynamic_slice(running, corner, (1, slices, side, side))
            running = lax.dynamic_update_slice(running, present + stacked[position][None], corner)
        return running

    return lax.fori_loop(0, slot_total, add_one, start_total)


def body(object_slices, probe_wave, offsets, counts, measured):
    slot_total = offsets.shape[0]
    pattern_side = probe_wave.shape[-1]
    half_side = pattern_side // 2
    step_size = step_gain / (
        jnp.max(probe_wave[0] * probe_wave[0] + probe_wave[1] * probe_wave[1]) + 1e-06
    )
    live_mask = (jnp.arange(slot_total, dtype=jnp.int32) < counts[0]).astype(jnp.float32)
    for iteration in range(ITERS):
        whole_band = lax.all_gather(object_slices, "scan", axis=2, tiled=True)
        extended = extended_2(whole_band, (("tile", 2),), half_side)
        accumulated = position_gradients(extended, probe_wave, offsets, measured, live_mask)
        band_total = extended.shape[2] - pattern_side
        middle = accumulated[:, :, half_side : half_side + band_total]
        rim_stack = jnp.concatenate(
            [accumulated[:, :, :half_side], accumulated[:, :, half_side + band_total :]], axis=2
        )
        returned = extended_2(rim_stack, (("tile", 2),), half_side)
        upper_rim = returned[:, :, :half_side]
        lower_rim = returned[:, :, returned.shape[2] - half_side :]
        middle = middle.at[:, :, :half_side].add(upper_rim)
        middle = middle.at[:, :, band_total - half_side :].add(lower_rim)
        gradient = lax.psum_scatter(middle, "scan", scatter_dimension=2, tiled=True)
        object_slices = object_slices - step_size * gradient
    return object_slices


def solution(mesh):
    placed = (
        P(None, None, ("tile", "scan"), None),
        P(),
        P(("tile", "scan"), None),
        P(("tile", "scan")),
        P(("tile", "scan"), None, None),
    )
    return jax.shard_map(
        body,
        mesh=mesh,
        in_specs=placed,
        out_specs=P(None, None, ("tile", "scan"), None),
        check_vma=False,
    )
```

profile of v0, /device:TPU:1, one launch (start us, length us, event | category | flops | bytes accessed | tf_op | source)
XLA Modules:
  0.0 451.6 jit_solution(4250984183810193176)
XLA Ops:
  6.5 31.1 %all_gather.6 = f32[2,4,64,256]{3,2,1,0:T(8,128)S(1)} all-gather(f32[2,4,8,256]{3,2,1,0:T(8,128)} %param.25), channel_id=1, replica_groups=mesh['tile'=64,'scan'=8] {'scan'}, dimensions={2}, use_global_device_ids=true | all-gather | bytes 589824 | tf_op jit(solution)/shard_map/all_gather | solution.py:143
  37.6 8.8 %collective-permute-start = (f32[2,4,64,256]{3,2,1,0:T(8,128)S(1)}, f32[2,4,64,256]{3,2,1,0:T(8,128)S(1)}, u32[]{:S(2)}, u32[]{:S(2)}) collective-permute-start(f32[2,4,64,256]{3,2,1,0:T(8,128)S(1)} %all_gather.6), channel_id=1, source_target_pairs={{0,8},{8,16},{16,24},{24,32},{32,40},{40,48},{48,56},{56,64},{64,7... | collective-permute-start | bytes 1572872 | tf_op jit(solution)/shard_map/ppermute | solution.py:23
  46.4 6.1 %collective-permute-start.1 = (f32[2,4,64,256]{3,2,1,0:T(8,128)S(1)}, f32[2,4,64,256]{3,2,1,0:T(8,128)S(1)}, u32[]{:S(2)}, u32[]{:S(2)}) collective-permute-start(f32[2,4,64,256]{3,2,1,0:T(8,128)S(1)} %all_gather.6), channel_id=1, source_target_pairs={{8,0},{16,8},{24,16},{32,24},{40,32},{48,40},{56,48},{64,56},{72,6... | collective-permute-start | bytes 1572872 | tf_op jit(solution)/shard_map/ppermute | solution.py:24
  55.6 6.9 %collective-permute-done.1 = f32[2,4,64,256]{3,2,1,0:T(8,128)S(1)} collective-permute-done((f32[2,4,64,256]{3,2,1,0:T(8,128)S(1)}, f32[2,4,64,256]{3,2,1,0:T(8,128)S(1)}, u32[]{:S(2)}, u32[]{:S(2)}) %collective-permute-start.1) | collective-permute-done | bytes 524320 | tf_op jit(solution)/shard_map/ppermute | solution.py:24
  62.7 4.2 while.40
  67.0 4.3 while.41
  100.0 23.8 %while.38 = (s32[]{:T(128)}, f32[2,4,192,256]{3,2,1,0:T(8,128)S(1)}, s32[2]{0:T(128)S(1)}, s32[2]{0:T(128)S(1)}, f32[2,4,128,128]{3,2,0,1:T(8,128)S(1)}, /*index...) while((s32[]{:T(128)}, f32[2,4,192,256]{3,2,1,0:T(8,128)S(1)}, ...), condition=%wide.region_2.3_spmd, body=%wide.region_1.2_spmd.sunk | while | flops 131080 | bytes 2621665 | solution.py:131
  105.6 3.1 dynamic_update_slice.32
  108.8 3.1 dynamic_update_slice.33
  117.5 3.1 dynamic_update_slice.32
  120.7 3.1 dynamic_update_slice.33
  123.9 2.1 collective-permute-start.2
  126.0 2.4 collective-permute-start.3
  128.4 9.3 %collective-permute-done.2 = f32[2,4,64,256]{3,2,1,0:T(8,128)S(1)} collective-permute-done((f32[2,4,64,256]{3,2,1,0:T(8,128)S(1)}, f32[2,4,64,256]{3,2,1,0:T(8,128)S(1)}, u32[]{:S(2)}, u32[]{:S(2)}) %collective-permute-start.2) | collective-permute-done | bytes 524320 | tf_op jit(solution)/shard_map/ppermute | solution.py:23
  137.7 4.4 collective-permute-done.3
  144.4 82.2 %reduce-scatter.3.cloned.1.call-done = f32[2,4,8,256]{3,2,1,0:T(8,128)} async-done(((f32[2,4,64,256]{3,2,1,0:T(8,128)}), f32[2,4,8,256]{3,2,1,0:T(8,128)}) %reduce-scatter.3.cloned.1.call-update) | async-done | bytes 65552 | tf_op jit(solution)/shard_map/reduce_scatter | solution.py:156
  227.5 29.0 %all_gather.7 = f32[2,4,64,256]{3,2,1,0:T(8,128)S(1)} all-gather(f32[2,4,8,256]{3,2,1,0:T(8,128)S(1)} %multiply_subtract_fusion.5), channel_id=1, replica_groups=mesh['tile'=64,'scan'=8] {'scan'}, dimensions={2}, use_global_device_ids=true | all-gather | bytes 589824 | tf_op jit(solution)/shard_map/all_gather | solution.py:143
  256.5 10.9 %collective-permute-start.4 = (f32[2,4,64,256]{3,2,1,0:T(8,128)S(1)}, f32[2,4,64,256]{3,2,1,0:T(8,128)S(1)}, u32[]{:S(2)}, u32[]{:S(2)}) collective-permute-start(f32[2,4,64,256]{3,2,1,0:T(8,128)S(1)} %all_gather.7), channel_id=1, source_target_pairs={{0,8},{8,16},{16,24},{24,32},{32,40},{40,48},{48,56},{56,64},{64,7... | collective-permute-start | bytes 1572872 | tf_op jit(solution)/shard_map/ppermute | solution.py:23
  267.4 1.9 collective-permute-start.5
  269.4 9.8 %collective-permute-done.4 = f32[2,4,64,256]{3,2,1,0:T(8,128)S(1)} collective-permute-done((f32[2,4,64,256]{3,2,1,0:T(8,128)S(1)}, f32[2,4,64,256]{3,2,1,0:T(8,128)S(1)}, u32[]{:S(2)}, u32[]{:S(2)}) %collective-permute-start.4) | collective-permute-done | bytes 524320 | tf_op jit(solution)/shard_map/ppermute | solution.py:23
  279.2 3.2 collective-permute-done.5
  282.7 4.2 while.42
  287.0 4.3 while.43
  319.8 24.0 %while.39 = (s32[]{:T(128)}, f32[2,4,192,256]{3,2,1,0:T(8,128)S(1)}, s32[2]{0:T(128)S(1)}, s32[2]{0:T(128)S(1)}, f32[2,4,128,128]{3,2,0,1:T(8,128)S(1)}, /*index...) while((s32[]{:T(128)}, f32[2,4,192,256]{3,2,1,0:T(8,128)S(1)}, ...), condition=%wide.region_5.6_spmd, body=%wide.region_4.5_spmd.sunk | while | flops 131080 | bytes 2621665 | solution.py:131
  325.5 3.1 dynamic_update_slice.34
  328.8 3.1 dynamic_update_slice.35
  337.4 3.1 dynamic_update_slice.34
  340.7 3.1 dynamic_update_slice.35
  343.9 1.9 collective-permute-start.6
  345.8 2.4 collective-permute-start.7
  348.2 9.3 %collective-permute-done.6 = f32[2,4,64,256]{3,2,1,0:T(8,128)S(1)} collective-permute-done((f32[2,4,64,256]{3,2,1,0:T(8,128)S(1)}, f32[2,4,64,256]{3,2,1,0:T(8,128)S(1)}, u32[]{:S(2)}, u32[]{:S(2)}) %collective-permute-start.6) | collective-permute-done | bytes 524320 | tf_op jit(solution)/shard_map/ppermute | solution.py:23
  359.5 83.5 %reduce-scatter.5.cloned.1.call-done = f32[2,4,8,256]{3,2,1,0:T(8,128)} async-done(((f32[2,4,64,256]{3,2,1,0:T(8,128)}), f32[2,4,8,256]{3,2,1,0:T(8,128)}) %reduce-scatter.5.cloned.1.call-update) | async-done | bytes 65552 | tf_op jit(solution)/shard_map/reduce_scatter | solution.py:156
  (217 shorter events, 88.0 us)
Async XLA Ops:
  6.5 47.5 %copy-start.3 = (s32[2,2]{1,0:T(2,128)S(1)}, s32[2,2]{1,0:T(2,128)}, u32[]{:S(2)}) copy-start(s32[2,2]{1,0:T(2,128)} %param.27) | copy-start | bytes 52
  6.5 49.0 %copy-start = (f32[2,128,128]{2,1,0:T(8,128)S(1)}, f32[2,128,128]{2,1,0:T(8,128)}, u32[]{:S(2)}) copy-start(f32[2,128,128]{2,1,0:T(8,128)} %param.26) | copy-start | bytes 393220
  6.5 220.1 %reduce-scatter.3.cloned.1.call-start = ((), (), s32[]{:S(2)}) async-start(), calls=%async_computation.2 | async-start | bytes 589824 | tf_op jit(solution)/shard_map/reduce_scatter | solution.py:156
  37.6 17.9 %collective-permute-start = (f32[2,4,64,256]{3,2,1,0:T(8,128)S(1)}, f32[2,4,64,256]{3,2,1,0:T(8,128)S(1)}, u32[]{:S(2)}, u32[]{:S(2)}) collective-permute-start(f32[2,4,64,256]{3,2,1,0:T(8,128)S(1)} %all_gather.6), channel_id=1, source_target_pairs={{0,8},{8,16},{16,24},{24,32},{32,40},{40,48},{48,56},{56,64},{64,7... | collective-permute-start | bytes 1572872 | tf_op jit(solution)/shard_map/ppermute | solution.py:23
  46.4 16.1 %collective-permute-start.1 = (f32[2,4,64,256]{3,2,1,0:T(8,128)S(1)}, f32[2,4,64,256]{3,2,1,0:T(8,128)S(1)}, u32[]{:S(2)}, u32[]{:S(2)}) collective-permute-start(f32[2,4,64,256]{3,2,1,0:T(8,128)S(1)} %all_gather.6), channel_id=1, source_target_pairs={{8,0},{16,8},{24,16},{32,24},{40,32},{48,40},{56,48},{64,56},{72,6... | collective-permute-start | bytes 1572872 | tf_op jit(solution)/shard_map/ppermute | solution.py:24
  80.5 4.3 copy-start.1
  123.9 102.8 %copy-start.2 = (f32[2,4,8,256]{3,2,1,0:T(8,128)S(1)}, f32[2,4,8,256]{3,2,1,0:T(8,128)}, u32[]{:S(2)}) copy-start(f32[2,4,8,256]{3,2,1,0:T(8,128)} %param.25) | copy-start | bytes 196612
  123.9 13.8 %collective-permute-start.2 = (f32[2,4,64,256]{3,2,1,0:T(8,128)S(1)}, f32[2,4,64,256]{3,2,1,0:T(8,128)S(1)}, u32[]{:S(2)}, u32[]{:S(2)}) collective-permute-start(f32[2,4,64,256]{3,2,1,0:T(8,128)S(1)} %get-tuple-element.431), channel_id=1, source_target_pairs={{0,8},{8,16},{16,24},{24,32},{32,40},{40,48},{48,56},{56,64},{64,7... | collective-permute-start | bytes 1572872 | tf_op jit(solution)/shard_map/ppermute | solution.py:23
  126.0 16.1 %collective-permute-start.3 = (f32[2,4,64,256]{3,2,1,0:T(8,128)S(1)}, f32[2,4,64,256]{3,2,1,0:T(8,128)S(1)}, u32[]{:S(2)}, u32[]{:S(2)}) collective-permute-start(f32[2,4,64,256]{3,2,1,0:T(8,128)S(1)} %get-tuple-element.432), channel_id=1, source_target_pairs={{8,0},{16,8},{24,16},{32,24},{40,32},{48,40},{56,48},{64,56},{72,6... | collective-permute-start | bytes 1572872 | tf_op jit(solution)/shard_map/ppermute | solution.py:24
  143.0 299.9 %reduce-scatter.5.cloned.1.call-start = ((), (), s32[]{:S(2)}) async-start(), calls=%async_computation.3 | async-start | bytes 589824 | tf_op jit(solution)/shard_map/reduce_scatter | solution.py:156
  256.5 22.7 %collective-permute-start.4 = (f32[2,4,64,256]{3,2,1,0:T(8,128)S(1)}, f32[2,4,64,256]{3,2,1,0:T(8,128)S(1)}, u32[]{:S(2)}, u32[]{:S(2)}) collective-permute-start(f32[2,4,64,256]{3,2,1,0:T(8,128)S(1)} %all_gather.7), channel_id=1, source_target_pairs={{0,8},{8,16},{16,24},{24,32},{32,40},{40,48},{48,56},{56,64},{64,7... | collective-permute-start | bytes 1572872 | tf_op jit(solution)/shard_map/ppermute | solution.py:23
  267.4 15.1 %collective-permute-start.5 = (f32[2,4,64,256]{3,2,1,0:T(8,128)S(1)}, f32[2,4,64,256]{3,2,1,0:T(8,128)S(1)}, u32[]{:S(2)}, u32[]{:S(2)}) collective-permute-start(f32[2,4,64,256]{3,2,1,0:T(8,128)S(1)} %all_gather.7), channel_id=1, source_target_pairs={{8,0},{16,8},{24,16},{32,24},{40,32},{48,40},{56,48},{64,56},{72,6... | collective-permute-start | bytes 1572872 | tf_op jit(solution)/shard_map/ppermute | solution.py:24
  343.9 13.7 %collective-permute-start.6 = (f32[2,4,64,256]{3,2,1,0:T(8,128)S(1)}, f32[2,4,64,256]{3,2,1,0:T(8,128)S(1)}, u32[]{:S(2)}, u32[]{:S(2)}) collective-permute-start(f32[2,4,64,256]{3,2,1,0:T(8,128)S(1)} %get-tuple-element.427), channel_id=1, source_target_pairs={{0,8},{8,16},{16,24},{24,32},{32,40},{40,48},{48,56},{56,64},{64,7... | collective-permute-start | bytes 1572872 | tf_op jit(solution)/shard_map/ppermute | solution.py:23
  345.8 12.8 %collective-permute-start.7 = (f32[2,4,64,256]{3,2,1,0:T(8,128)S(1)}, f32[2,4,64,256]{3,2,1,0:T(8,128)S(1)}, u32[]{:S(2)}, u32[]{:S(2)}) collective-permute-start(f32[2,4,64,256]{3,2,1,0:T(8,128)S(1)} %get-tuple-element.428), channel_id=1, source_target_pairs={{8,0},{16,8},{24,16},{32,24},{40,32},{48,40},{56,48},{64,56},{72,6... | collective-permute-start | bytes 1572872 | tf_op jit(solution)/shard_map/ppermute | solution.py:24
Sparse Core Ops, SparseCore 0:
  143.2 83.4 reduce-scatter.2
  359.7 83.2 reduce-scatter.4
where the time goes:
time: 456 us; the launch traced here: 452 us
  waiting for transfers between devices  210 us (46%)
  blocking collectives  60.1 us (13%)
  matrix products  57.7 us (13%)
  local copies, waits for them, and re-layouts  47.5 us (10%)
  starting transfers between devices  36.6 us (8%)
  loops' own time  17.2 us (4%)
  between operations  16.3 us (4%)
  other arithmetic  6.38 us (1%)
    reduce_scatter x2, waiting for transfers between devices, body(): gradient = lax.psum_scatter(middle, 'scan', scatter_dimension=2, tiled=True)  166 us
    all_gather x2, blocking collectives, body(): whole_band = lax.all_gather(object_slices, 'scan', axis=2, tiled=True)  60.1 us
    ppermute x4, waiting for transfers between devices, extended_2(): before = lax.ppermute(last, axis, up)  28.5 us
    dot_general x64, matrix products, apply_left(): jnp.einsum('ij,pjk->pik', matrix, field, precision=highest, preferred_ele...  28.1 us
    dot_general x64, matrix products, apply_right(): jnp.einsum('pik,lk->pil', field, matrix, precision=highest, preferred_ele...  27.7 us
    dynamic_update_slice x8, local copies, waits for them, and re-layouts, add_one(): lax.dynamic_update_slice(running, present + stacked[position][None], corner)  24.7 us
    ppermute x4, starting transfers between devices, extended_2(): before = lax.ppermute(last, axis, up)  23.8 us
    another operation x2, loops' own time, position_gradients(): return lax.fori_loop(0, slot_total, add_one, start_total)  16.6 us
  transfers between devices with their start and end apart: 10, of which 9 were waited for; matrix products, arithmetic and copies ran while one was open for 1% of the time, Pallas kernels for 0%

commit v1 on v0

v1 whole, which is shorter than its diff:
```python
import functools

import jax
import jax.numpy as jnp
import ml_dtypes
import numpy as np
from jax import lax
from jax.experimental import pallas as pl
from jax.experimental.pallas import tpu as pltpu
from jax.sharding import PartitionSpec as P


ITERS = 2
S = 4
W = 128
SCAN = 8
ROWS = 8
PROP, PROP_C, DFT, DFT_C = range(4)
MESH = pl.DeviceIdType.MESH
F32 = jnp.float32
BF16 = jnp.bfloat16
VMEM_BYTES = 48 * 2**20


def tables():
    n = np.arange(W)
    dft = np.exp(-2j * np.pi * (n[:, None] * n[None, :] % W) / W) / np.sqrt(W)
    freq = (n + W // 2) % W - W // 2
    prop = np.conj(dft) @ (np.exp(-1j * np.pi * freq * freq / (2.0 * W))[:, None] * dft)
    lefts, rights = [], []
    for m in (prop, np.conj(prop), dft, np.conj(dft)):
        right = np.block([[m.real, m.imag], [-m.imag, m.real]])
        left = np.block([[m.real, -m.imag], [m.imag, m.real]])
        for big, out, axis in ((right, rights, 0), (left, lefts, 1)):
            high = big.astype(ml_dtypes.bfloat16)
            low = (big - high.astype(np.float64)).astype(ml_dtypes.bfloat16)
            out.append(np.concatenate([high, high, low], axis=axis))
    return np.stack(lefts), np.stack(rights)


def halves(value):
    high = value.astype(BF16)
    return high, (value - high.astype(F32)).astype(BF16)


def sandwich(re, im, left_ref, right_ref, which):
    high, low = halves(jnp.concatenate([re, im], axis=0))
    mid = jnp.dot(left_ref[which], jnp.concatenate([high, low, high], axis=0), preferred_element_type=F32)
    high, low = halves(jnp.concatenate([mid[:W], mid[W:]], axis=1))
    out = jnp.dot(jnp.concatenate([high, low, high], axis=1), right_ref[which], preferred_element_type=F32)
    return out[:, :W], out[:, W:]


def mul(a, b):
    return a[0] * b[0] - a[1] * b[1], a[0] * b[1] + a[1] * b[0]


def mul_conj(a, b):
    return a[0] * b[0] + a[1] * b[1], a[0] * b[1] - a[1] * b[0]


def shifted(value, amount, axis):
    for bit in range(7):
        moved = pltpu.roll(value, 1 << bit, axis)
        value = jnp.where(lax.rem(lax.div(amount, 1 << bit), 2) == 1, moved, value)
    return value


def kernel(
    tiles, offsets_ref, counts_ref, object_ref, probe_ref, measured_ref, lefts_ref, rights_ref, out_ref,
    obj, probe, shift_probe, meas, meas_in, left, right, meta_out, meta, jobs, patch, gather_out, grad, grad_in,
    part, cross_in, last_in, near_send, near_recv, meta_send, meta_recv, meas_send, meas_recv, gather_send,
    gather_recv, reduce_send, reduce_recv, cross_send, cross_recv, last_send, last_recv, local_sem,
):
    tile = lax.axis_index("tile")
    me = lax.axis_index("scan")
    group = [(tile, lax.rem(me + j, SCAN)) for j in range(SCAN)]
    source = [lax.rem(me + SCAN - j, SCAN) for j in range(SCAN)]
    around = {d: (lax.rem(tile + d + tiles, tiles), me) for d in (-2, -1, 1, 2)}
    my_rows = pl.ds(pl.multiple_of(me * ROWS, ROWS), ROWS)

    barrier = pltpu.get_barrier_semaphore()
    for device in group[1:] + list(around.values()):
        pl.semaphore_signal(barrier, inc=1, device_id=device, device_id_type=MESH)

    locals_ = [
        pltpu.make_async_copy(object_ref, obj.at[1], local_sem.at[0]),
        pltpu.make_async_copy(probe_ref, probe, local_sem.at[1]),
        pltpu.make_async_copy(measured_ref.at[0], meas, local_sem.at[2]),
        pltpu.make_async_copy(lefts_ref, left, local_sem.at[3]),
        pltpu.make_async_copy(rights_ref, right, local_sem.at[4]),
    ]
    for copy in locals_:
        copy.start()

    row = lax.broadcasted_iota(jnp.int32, (ROWS, W), 0)
    lane = lax.broadcasted_iota(jnp.int32, (ROWS, W), 1)
    fields = [counts_ref[0], offsets_ref[0, 0], offsets_ref[0, 1], offsets_ref[1, 0], offsets_ref[1, 1]]
    packed = jnp.zeros((ROWS, W), jnp.int32)
    for f, field in enumerate(fields):
        packed = jnp.where(row == f, field, packed)
    meta_out[...] = packed
    meta[me] = packed

    pl.semaphore_wait(barrier, SCAN - 1 + 4)

    def send(src, dst, send_sem, recv_sem, device):
        copy = pltpu.make_async_remote_copy(
            src_ref=src, dst_ref=dst, send_sem=send_sem, recv_sem=recv_sem, device_id=device, device_id_type=MESH
        )
        copy.start()
        return copy

    sends = []
    meta_copies = [
        send(meta_out, meta.at[me], meta_send.at[j - 1], meta_recv.at[j - 1], group[j]) for j in range(1, SCAN)
    ]
    near_copies = []
    for k in range(S):
        near_copies.append(
            [
                send(object_ref.at[:, k], obj.at[0, :, k], near_send.at[k, 0], near_recv.at[k, 0], around[1]),
                send(object_ref.at[:, k], obj.at[2, :, k], near_send.at[k, 1], near_recv.at[k, 1], around[-1]),
            ]
        )
    locals_[1].wait()
    intensity = probe[0] * probe[0] + probe[1] * probe[1]
    step = 0.5 / (jnp.max(intensity, keepdims=True) + 1e-06)

    for copy in meta_copies:
        copy.wait_recv()
    seen = [[meta[s, f : f + 1, :] for f in range(5)] for s in range(SCAN)]
    count = jnp.zeros((ROWS, W), jnp.int32)
    first_row = first_col = second_row = second_col = empty_rank = count
    empties = jnp.zeros((1, W), jnp.int32)
    for s in range(SCAN):
        here = row == s
        count = jnp.where(here, seen[s][0], count)
        first_row = jnp.where(here, seen[s][1], first_row)
        first_col = jnp.where(here, seen[s][2], first_col)
        empty_rank = jnp.where(here, empties, empty_rank)
        empties = empties + jnp.where(seen[s][0] == 0, 1, 0)
    takes = []
    doubles = jnp.zeros((1, W), jnp.int32)
    for s in range(SCAN):
        match = jnp.where((seen[s][0] == 2) & (doubles == empty_rank) & (count == 0), 1, 0)
        doubles = doubles + jnp.where(seen[s][0] == 2, 1, 0)
        jobs[2 + s] = match
        second_row = jnp.where(match == 1, seen[s][3], second_row)
        second_col = jnp.where(match == 1, seen[s][4], second_col)
    jobs[0] = jnp.where(count == 0, second_row, first_row)
    jobs[1] = jnp.where(count == 0, second_col, first_col)

    def masks(s):
        wide = jnp.broadcast_to(jobs[1, pl.ds(s, 1), :], (ROWS, W))
        tall = jnp.broadcast_to(jobs[0, pl.ds(s, 1), :], (ROWS, W))
        return lane >= wide, tall

    job_masks = [masks(group[j][1]) for j in range(SCAN)]
    before_masks = [me * ROWS + row >= tall for _, tall in job_masks]

    def gather(it, k):
        bands = [[[obj[b, p, k, :, h * W : (h + 1) * W] for h in range(2)] for p in range(2)] for b in range(3)]
        for j in range(SCAN):
            left_part = job_masks[j][0]
            for p in range(2):
                prev, own, after = [jnp.where(left_part, bands[b][p][0], bands[b][p][1]) for b in range(3)]
                merged = jnp.where(before_masks[j], prev, after)
                if j == 0:
                    patch[it, k, p, 0, my_rows, :] = merged
                    patch[it, k, p, 1, my_rows, :] = own
                else:
                    gather_out[it, k, j - 1, p, 0] = merged
                    gather_out[it, k, j - 1, p, 1] = own
            if j:
                send(
                    gather_out.at[it, k, j - 1],
                    patch.at[it, k, :, :, my_rows, :],
                    gather_send.at[it, k, j - 1],
                    gather_recv.at[it, k, j - 1],
                    group[j],
                )

    def gather_wait(it, k):
        for j in range(1, SCAN):
            pltpu.make_async_remote_copy(
                src_ref=gather_out.at[it, k, j - 1],
                dst_ref=patch.at[it, k, :, :, pl.ds(pl.multiple_of(source[j] * ROWS, ROWS), ROWS), :],
                send_sem=gather_send.at[it, k, j - 1],
                recv_sem=gather_recv.at[it, k, j - 1],
                device_id=group[j],
                device_id_type=MESH,
            ).wait_recv()

    locals_[0].wait()
    for k in range(S):
        for copy in near_copies[k]:
            copy.wait_recv()
        gather(0, k)
    meas_copies = [
        send(measured_ref.at[1], meas_in.at[j - 1], meas_send.at[j - 1], meas_recv.at[j - 1], group[j])
        for j in range(1, SCAN)
    ]

    my_row = jobs[0, pl.ds(me, 1), :]
    my_col = jobs[1, pl.ds(me, 1), :]
    for p in range(2):
        shift_probe[p] = shifted(shifted(probe[p], my_row, 0), my_col, 1)
    locals_[2].wait()
    locals_[3].wait()
    locals_[4].wait()

    for it in range(ITERS):
        final = it == ITERS - 1

        def fetch(k):
            gather_wait(it, k)
            return patch[it, k, 0].reshape(W, W), patch[it, k, 1].reshape(W, W)

        def reduce_send_all(k, value):
            for p in range(2):
                grad[it, k, p] = value[p].reshape(2, W // 2, W)
            for j in range(1, SCAN):
                rows = pl.ds(pl.multiple_of(group[j][1] * ROWS, ROWS), ROWS)
                send(
                    grad.at[it, k, :, :, rows, :],
                    grad_in.at[it, k, j - 1],
                    reduce_send.at[it, k, j - 1],
                    reduce_recv.at[it, k, j - 1],
                    group[j],
                )

        shone = (shift_probe[0], shift_probe[1])
        arrived = [shone]
        patches = [fetch(0)]
        wave = mul(shone, patches[0])
        for k in range(1, S):
            arrived.append(sandwich(*wave, left, right, PROP))
            patches.append(fetch(k))
            wave = mul(arrived[k], patches[k])
        far = sandwich(*wave, left, right, DFT)
        if it == 0:
            value = meas[...]
            for j in range(1, SCAN):
                meas_copies[j - 1].wait_recv()
                take = jobs[pl.ds(2 + source[j], 1), pl.ds(me, 1), :].reshape(1, W)
                value = jnp.where(take == 1, meas_in[j - 1], value)
            meas[...] = value
        ratio = meas[...] * lax.rsqrt(jnp.maximum(far[0] * far[0] + far[1] * far[1], 0.04))
        back = sandwich(far[0] - ratio * far[0], far[1] - ratio * far[1], left, right, DFT_C)
        for k in range(S - 1, 0, -1):
            reduce_send_all(k, mul_conj(arrived[k], back))
            back = sandwich(*mul_conj(patches[k], back), left, right, PROP_C)
        reduce_send_all(0, mul_conj(shone, back))

        for k in range(S - 1, -1, -1):
            zero = jnp.zeros((ROWS, W), F32)
            total = [[[zero, zero] for p in range(2)] for b in range(3)]
            for j in range(SCAN):
                sender = lax.rem(me + SCAN - j, SCAN)
                left_part, tall = masks(sender)
                before = me * ROWS + row >= tall
                if j:
                    pltpu.make_async_remote_copy(
                        src_ref=grad.at[it, k, :, :, my_rows, :],
                        dst_ref=grad_in.at[it, k, j - 1],
                        send_sem=reduce_send.at[it, k, j - 1],
                        recv_sem=reduce_recv.at[it, k, j - 1],
                        device_id=group[j],
                        device_id_type=MESH,
                    ).wait_recv()
                for p in range(2):
                    if j:
                        merged, own = grad_in[it, k, j - 1, p, 0], grad_in[it, k, j - 1, p, 1]
                    else:
                        merged, own = grad[it, k, p, 0, my_rows, :], grad[it, k, p, 1, my_rows, :]
                    for b, term in ((0, jnp.where(before, merged, 0.0)), (1, own), (2, jnp.where(before, 0.0, merged))):
                        total[b][p][0] = total[b][p][0] + jnp.where(left_part, term, 0.0)
                        total[b][p][1] = total[b][p][1] + jnp.where(left_part, 0.0, term)
            for b in range(3):
                for p in range(2):
                    for h in range(2):
                        part[it, k, b, p, :, h * W : (h + 1) * W] = total[b][p][h]
            if final:
                for n, (d, b) in enumerate(((1, 2), (-1, 0))):
                    send(part.at[it, k, b], last_in.at[k, n], last_send.at[k, n], last_recv.at[k, n], around[d])
            else:
                for n, (d, b, w) in enumerate(((1, 1, 2), (-1, 0, 2), (2, 2, 1), (-2, 0, 1))):
                    send(
                        part.at[it, k, pl.ds(b, w)],
                        cross_in.at[k, pl.ds((0, 2, 4, 5)[n], w)],
                        cross_send.at[k, n],
                        cross_recv.at[k, n],
                        around[d],
                    )

        for k in range(S - 1, -1, -1):
            if final:
                for n, (d, b) in enumerate(((1, 2), (-1, 0))):
                    pltpu.make_async_remote_copy(
                        src_ref=part.at[it, k, b], dst_ref=last_in.at[k, n], send_sem=last_send.at[k, n],
                        recv_sem=last_recv.at[k, n], device_id=around[d], device_id_type=MESH,
                    ).wait_recv()
                for p in range(2):
                    gradient = part[it, k, 1, p] + last_in[k, 0, p] + last_in[k, 1, p]
                    out_ref[p, k] = obj[1, p, k] - step * gradient
            else:
                for n, (d, b, w) in enumerate(((1, 1, 2), (-1, 0, 2), (2, 2, 1), (-2, 0, 1))):
                    pltpu.make_async_remote_copy(
                        src_ref=part.at[it, k, pl.ds(b, w)], dst_ref=cross_in.at[k, pl.ds((0, 2, 4, 5)[n], w)],
                        send_sem=cross_send.at[k, n], recv_sem=cross_recv.at[k, n], device_id=around[d],
                        device_id_type=MESH,
                    ).wait_recv()
                for b, (one, two) in enumerate(((0, 4), (1, 2), (3, 5))):
                    for p in range(2):
                        gradient = part[it, k, b, p] + cross_in[k, one, p] + cross_in[k, two, p]
                        obj[b, p, k] = obj[b, p, k] - step * gradient
                gather(it + 1, k)

    for copy in meta_copies + meas_copies + [copy for pair in near_copies for copy in pair]:
        copy.wait_send()
    for it in range(ITERS):
        for k in range(S):
            for j in range(1, SCAN):
                pltpu.make_async_copy(
                    gather_out.at[it, k, j - 1], gather_out.at[it, k, j - 1], gather_send.at[it, k, j - 1]
                ).wait()
                pltpu.make_async_copy(
                    grad_in.at[it, k, j - 1], grad_in.at[it, k, j - 1], reduce_send.at[it, k, j - 1]
                ).wait()
    for k in range(S):
        for n, w in enumerate((2, 2, 1, 1)):
            pltpu.make_async_copy(part.at[0, k, pl.ds(0, w)], part.at[0, k, pl.ds(0, w)], cross_send.at[k, n]).wait()
        for n in range(2):
            pltpu.make_async_copy(part.at[1, k, 0], part.at[1, k, 0], last_send.at[k, n]).wait()


def body(tiles, object_slices, probe_wave, offsets, counts, measured):
    lefts, rights = tables()
    peers = SCAN - 1
    dma = pltpu.SemaphoreType.DMA
    any_space = pl.BlockSpec(memory_space=pl.ANY)
    smem = pl.BlockSpec(memory_space=pltpu.SMEM)
    scratch = [
        pltpu.VMEM((3, 2, S, ROWS, 2 * W), F32),
        pltpu.VMEM((2, W, W), F32),
        pltpu.VMEM((2, W, W), F32),
        pltpu.VMEM((W, W), F32),
        pltpu.VMEM((peers, W, W), F32),
        pltpu.VMEM(lefts.shape, BF16),
        pltpu.VMEM(rights.shape, BF16),
        pltpu.VMEM((ROWS, W), jnp.int32),
        pltpu.VMEM((SCAN, ROWS, W), jnp.int32),
        pltpu.VMEM((2 + SCAN, ROWS, W), jnp.int32),
        pltpu.VMEM((ITERS, S, 2, 2, W // 2, W), F32),
        pltpu.VMEM((ITERS, S, peers, 2, 2, ROWS, W), F32),
        pltpu.VMEM((ITERS, S, 2, 2, W // 2, W), F32),
        pltpu.VMEM((ITERS, S, peers, 2, 2, ROWS, W), F32),
        pltpu.VMEM((ITERS, S, 3, 2, ROWS, 2 * W), F32),
        pltpu.VMEM((S, 6, 2, ROWS, 2 * W), F32),
        pltpu.VMEM((S, 2, 2, ROWS, 2 * W), F32),
    ]
    for shape in ((S, 2), (peers,), (peers,), (ITERS, S, peers), (ITERS, S, peers), (S, 4), (S, 2)):
        scratch += [dma(shape), dma(shape)]
    scratch.append(dma((5,)))
    return pl.pallas_call(
        functools.partial(kernel, tiles),
        out_shape=jax.ShapeDtypeStruct(object_slices.shape, F32),
        in_specs=[smem, smem] + [any_space] * 5,
        out_specs=pl.BlockSpec(memory_space=pltpu.VMEM),
        scratch_shapes=scratch,
        compiler_params=pltpu.CompilerParams(
            collective_id=0, has_side_effects=True, vmem_limit_bytes=VMEM_BYTES
        ),
    )(offsets, counts, object_slices, probe_wave, measured, jnp.asarray(lefts), jnp.asarray(rights))


def solution(mesh):
    placed = (
        P(None, None, ("tile", "scan"), None),
        P(),
        P(("tile", "scan"), None),
        P(("tile", "scan")),
        P(("tile", "scan"), None, None),
    )
    return jax.shard_map(
        functools.partial(body, mesh.shape["tile"]),
        mesh=mesh,
        in_specs=placed,
        out_specs=P(None, None, ("tile", "scan"), None),
        check_vma=False,
    )
```

time: 456 us -> 78.9 us (0.17)
  the two profiles are of different devices: /device:TPU:1 before, /device:TPU:105 now
where the time goes in v1:
time: 78.9 us; the launch traced here: 78.7 us
  Pallas kernels  71.2 us (90%)
  local copies, waits for them, and re-layouts  6.77 us (9%)
    pallas_call x1, Pallas kernels, body(): pl.pallas_call(functools.partial(kernel, tiles), out_shape=jax.ShapeDtype...  71.2 us
    unnamed x13, local copies, waits for them, and re-layouts  6.77 us

profile of v1, /device:TPU:105, one launch (start us, length us, event | category | flops | bytes accessed | tf_op | source)
XLA Modules:
  0.0 78.7 jit_solution(946395125726745314)
XLA Ops:
  0.7 0.0 copy-start
  0.7 1.4 %copy-done = bf16[4,768,256]{2,1,0:T(8,128)(2,1)S(1)} copy-done((bf16[4,768,256]{2,1,0:T(8,128)(2,1)S(1)}, bf16[4,768,256]{2,1,0:T(8,128)(2,1)}, u32[]{:S(2)}) %copy-start) | copy-done | bytes 1572888
  2.1 0.0 copy-start.1
  2.1 1.4 %copy-done.1 = bf16[4,256,768]{2,1,0:T(8,128)(2,1)S(1)} copy-done((bf16[4,256,768]{2,1,0:T(8,128)(2,1)S(1)}, bf16[4,256,768]{2,1,0:T(8,128)(2,1)}, u32[]{:S(2)}) %copy-start.1) | copy-done | bytes 1572888
  3.5 0.0 copy-start.2
  3.5 0.9 %copy-done.2 = f32[2,128,128]{2,1,0:T(8,128)S(1)} copy-done((f32[2,128,128]{2,1,0:T(8,128)S(1)}, f32[2,128,128]{2,1,0:T(8,128)}, u32[]{:S(2)}) %copy-start.2) | copy-done | bytes 131096
  4.4 0.0 copy-start.3
  4.4 0.9 %copy-done.3 = f32[2,128,128]{2,1,0:T(8,128)S(1)} copy-done((f32[2,128,128]{2,1,0:T(8,128)S(1)}, f32[2,128,128]{2,1,0:T(8,128)}, u32[]{:S(2)}) %copy-start.3) | copy-done | bytes 131096
  5.3 0.0 copy-start.4
  5.3 0.8 %copy-done.4 = f32[2,4,8,256]{3,2,1,0:T(8,128)S(1)} copy-done((f32[2,4,8,256]{3,2,1,0:T(8,128)S(1)}, f32[2,4,8,256]{3,2,1,0:T(8,128)}, u32[]{:S(2)}) %copy-start.4) | copy-done | bytes 65560
  6.1 0.0 copy-start.5
  6.1 0.7 copy-done.5
  6.8 71.2 %shard_map.73 = f32[2,4,8,256]{3,2,1,0:T(8,128)S(1)} custom-call(s32[2,2]{1,0:T(2,128)S(1)} %copy-done.5, s32[1]{0:T(128)S(6)} %copy.9.counts_ref, f32[2,4,8,256]{3,2,1,0:T(8,128)S(1)} %copy-done.4, f32[2,128,128]{2,1,0:T(8,128)S(1)} %copy-done.2, f32[2,128,128]{2,1,0:T(8,128)S(1)} %copy-done.3, bf16[4,256,768]{2,1,0:T(8,128)(2,1)S(1)} %copy-done.1, ...), custom_call_target="tpu_custom_call" | custom-call | tf_op jit(solution)/shard_map/pallas_call | solution.py:366
  78.0 0.6 copy.10
Async XLA Ops:
  0.7 1.4 %copy-start = (bf16[4,768,256]{2,1,0:T(8,128)(2,1)S(1)}, bf16[4,768,256]{2,1,0:T(8,128)(2,1)}, u32[]{:S(2)}) copy-start(bf16[4,768,256]{2,1,0:T(8,128)(2,1)} %constant.5.clone.rights_ref) | copy-start | bytes 4718596
  2.1 1.4 %copy-start.1 = (bf16[4,256,768]{2,1,0:T(8,128)(2,1)S(1)}, bf16[4,256,768]{2,1,0:T(8,128)(2,1)}, u32[]{:S(2)}) copy-start(bf16[4,256,768]{2,1,0:T(8,128)(2,1)} %constant.4.clone.lefts_ref) | copy-start | bytes 4718596
  3.5 0.9 %copy-start.2 = (f32[2,128,128]{2,1,0:T(8,128)S(1)}, f32[2,128,128]{2,1,0:T(8,128)}, u32[]{:S(2)}) copy-start(f32[2,128,128]{2,1,0:T(8,128)} %probe_ref.1) | copy-start | bytes 393220
  4.4 0.9 %copy-start.3 = (f32[2,128,128]{2,1,0:T(8,128)S(1)}, f32[2,128,128]{2,1,0:T(8,128)}, u32[]{:S(2)}) copy-start(f32[2,128,128]{2,1,0:T(8,128)} %measured_ref.1) | copy-start | bytes 393220
  5.3 0.8 %copy-start.4 = (f32[2,4,8,256]{3,2,1,0:T(8,128)S(1)}, f32[2,4,8,256]{3,2,1,0:T(8,128)}, u32[]{:S(2)}) copy-start(f32[2,4,8,256]{3,2,1,0:T(8,128)} %object_ref.1) | copy-start | bytes 196612
  6.1 0.7 copy-start.5

commit v2 on v1

v2 whole, which is shorter than its diff:
```python
import functools

import jax
import jax.numpy as jnp
import ml_dtypes
import numpy as np
from jax import lax
from jax.experimental import pallas as pl
from jax.experimental.pallas import tpu as pltpu
from jax.sharding import PartitionSpec as P


ITERS = 2
S = 4
W = 128
SCAN = 8
ROWS = 8
PROP, PROP_C, DFT, DFT_C = range(4)
MESH = pl.DeviceIdType.MESH
F32 = jnp.float32
BF16 = jnp.bfloat16
VMEM_BYTES = 60 * 2**20


def tables():
    n = np.arange(W)
    dft = np.exp(-2j * np.pi * (n[:, None] * n[None, :] % W) / W) / np.sqrt(W)
    freq = (n + W // 2) % W - W // 2
    prop = np.conj(dft) @ (np.exp(-1j * np.pi * freq * freq / (2.0 * W))[:, None] * dft)
    lefts, rights = [], []
    for m in (prop, np.conj(prop), dft, np.conj(dft)):
        right = np.block([[m.real, m.imag], [-m.imag, m.real]])
        left = np.block([[m.real, -m.imag], [m.imag, m.real]])
        for big, out, axis in ((right, rights, 0), (left, lefts, 1)):
            high = big.astype(ml_dtypes.bfloat16)
            low = (big - high.astype(np.float64)).astype(ml_dtypes.bfloat16)
            out.append(np.concatenate([high, high, low], axis=axis))
    return np.stack(lefts), np.stack(rights)


def halves(value):
    high = value.astype(BF16)
    return high, (value - high.astype(F32)).astype(BF16)


def sandwich(re, im, left_ref, right_ref, which):
    high, low = halves(jnp.concatenate([re, im], axis=0))
    mid = jnp.dot(left_ref[which], jnp.concatenate([high, low, high], axis=0), preferred_element_type=F32)
    high, low = halves(jnp.concatenate([mid[:W], mid[W:]], axis=1))
    out = jnp.dot(jnp.concatenate([high, low, high], axis=1), right_ref[which], preferred_element_type=F32)
    return out[:, :W], out[:, W:]


def mul(a, b):
    return a[0] * b[0] - a[1] * b[1], a[0] * b[1] + a[1] * b[0]


def mul_conj(a, b):
    return a[0] * b[0] + a[1] * b[1], a[0] * b[1] - a[1] * b[0]


def shifted(value, amount, axis):
    for bit in range(7):
        moved = pltpu.roll(value, 1 << bit, axis)
        value = jnp.where(lax.rem(lax.div(amount, 1 << bit), 2) == 1, moved, value)
    return value

class Links:
    def __init__(self, sems):
        self.sems = sems
        self.started = []
        self.open = {}

    def send(self, name, index, src, dst, device, own=None):
        send_sem, recv_sem = self.sems[name]
        copy = pltpu.make_async_remote_copy(
            src_ref=src, dst_ref=dst, send_sem=send_sem.at[index], recv_sem=recv_sem.at[index], device_id=device,
            device_id_type=MESH,
        )
        if own is None:
            copy.start()
        else:
            pl.when(own)(lambda: pltpu.make_async_copy(src, dst, recv_sem.at[index]).start())
            pl.when(jnp.logical_not(own))(copy.start)
        self.started.append((copy, own))
        self.open[name, index] = copy

    def receive(self, name, index, dst=None):
        copy = self.open.pop((name, index))
        if dst is not None:
            copy = pltpu.make_async_remote_copy(
                src_ref=copy.src_ref, dst_ref=dst, send_sem=copy.src_sem, recv_sem=copy.dst_sem,
                device_id=copy.device_id, device_id_type=MESH,
            )
        copy.wait_recv()

    def finish(self):
        for copy, own in self.started:
            if own is None:
                copy.wait_send()
        if any(own is not None for _, own in self.started):
            own = [own for _, own in self.started if own is not None][0]

            @pl.when(jnp.logical_not(own))
            def _():
                for copy, own in self.started:
                    if own is not None:
                        copy.wait_send()


CROSS = ((1, 1, 2, 0), (-1, 0, 2, 2), (2, 2, 1, 4), (-2, 0, 1, 5))
LAST = ((1, 2), (-1, 0))


def twin(tile, scan):
    core, half = lax.rem(tile, 2), lax.div(scan, 4)
    return tile - core + half, lax.rem(scan, 4) + 4 * core


def kernel(
    tiles, names, offsets_hbm, counts_hbm, object_hbm, probe_hbm, measured_hbm, lefts_hbm, rights_hbm, out_ref,
    offsets_ref, counts_ref, obj, obj_work, out_base, probe, shift_probe, meas, meas_in, left, right, meta_out,
    meta_own, meta_work, jobs_own, jobs_work, patch, gather_out, grad, grad_in, part, cross_in, last_in, local_sem,
    *sems,
):
    links = Links({name: (sems[2 * i], sems[2 * i + 1]) for i, name in enumerate(names)})
    tile = lax.axis_index("tile")
    me = lax.axis_index("scan")
    region, member = twin(tile, me)
    same = region == tile

    def ring(first, j):
        return lax.rem(first + j + SCAN, SCAN)

    owners = [(tile, ring(me, j)) for j in range(SCAN)]
    workers = [twin(tile, ring(me, j)) for j in range(SCAN)]
    members = [twin(region, ring(member, j)) for j in range(SCAN)]
    region_owners = [(region, ring(member, j)) for j in range(SCAN)]
    near = {d: (lax.rem(tile + d + tiles, tiles), me) for d in (-1, 1)}
    around = {d: twin(lax.rem(region + d + tiles, tiles), member) for d in (-2, -1, 1, 2)}

    def rows_of(s):
        return pl.ds(pl.multiple_of(s * ROWS, ROWS), ROWS)

    barrier = pltpu.get_barrier_semaphore()
    others = owners[1:] + workers[1:] + members[1:] + region_owners[1:] + list(near.values()) + list(around.values())
    for device in others:
        pl.semaphore_signal(barrier, inc=1, device_id=device, device_id_type=MESH)

    @pl.when(jnp.logical_not(same))
    def _():
        pl.semaphore_signal(barrier, inc=1, device_id=workers[0], device_id_type=MESH)

    local = {}
    for n, (name, src, dst) in enumerate(
        (
            ("offsets", offsets_hbm, offsets_ref),
            ("counts", counts_hbm, counts_ref),
            ("probe", probe_hbm, probe),
            ("object", object_hbm, obj.at[1]),
            ("lefts", lefts_hbm, left),
            ("rights", rights_hbm, right),
        )
    ):
        local[name] = pltpu.make_async_copy(src, dst, local_sem.at[n])
        local[name].start()

    row = lax.broadcasted_iota(jnp.int32, (ROWS, W), 0)
    lane = lax.broadcasted_iota(jnp.int32, (ROWS, W), 1)
    local.pop("offsets").wait()
    local.pop("counts").wait()
    fields = [counts_ref[0], offsets_ref[0, 0], offsets_ref[0, 1], offsets_ref[1, 0], offsets_ref[1, 1]]
    packed = jnp.zeros((ROWS, W), jnp.int32)
    for f, field in enumerate(fields):
        packed = jnp.where(row == f, field, packed)
    meta_out[...] = packed
    meta_own[me] = packed

    pl.semaphore_wait(barrier, len(others) + jnp.where(same, 0, 1))

    for j in range(1, SCAN):
        links.send("meta_own", (j - 1,), meta_out, meta_own.at[me], owners[j])
    for j in range(SCAN):
        links.send("meta_work", (j,), meta_out, meta_work.at[me], workers[j], None if j else same)
    for k in range(S):
        links.send("near", (k, 0), object_hbm.at[:, k], obj.at[0, :, k], near[1])
        links.send("near", (k, 1), object_hbm.at[:, k], obj.at[2, :, k], near[-1])
    links.send("meas", (0,), measured_hbm.at[0], meas_in.at[0], workers[0], same)
    for j in range(1, SCAN):
        links.send("meas", (j,), measured_hbm.at[1], meas_in.at[j], workers[j])
    local.pop("probe").wait()
    intensity = probe[0] * probe[0] + probe[1] * probe[1]
    step = 0.5 / (jnp.max(intensity, keepdims=True) + 1e-06)

    def assign(meta, jobs):
        seen = [[meta[s, f : f + 1, :] for f in range(5)] for s in range(SCAN)]
        count = jnp.zeros((ROWS, W), jnp.int32)
        first_row = first_col = second_row = second_col = empty_rank = count
        empties = jnp.zeros((1, W), jnp.int32)
        for s in range(SCAN):
            here = row == s
            count = jnp.where(here, seen[s][0], count)
            first_row = jnp.where(here, seen[s][1], first_row)
            first_col = jnp.where(here, seen[s][2], first_col)
            empty_rank = jnp.where(here, empties, empty_rank)
            empties = empties + jnp.where(seen[s][0] == 0, 1, 0)
        doubles = jnp.zeros((1, W), jnp.int32)
        for s in range(SCAN):
            match = jnp.where((seen[s][0] == 2) & (doubles == empty_rank) & (count == 0), 1, 0)
            doubles = doubles + jnp.where(seen[s][0] == 2, 1, 0)
            jobs[2 + s] = match
            second_row = jnp.where(match == 1, seen[s][3], second_row)
            second_col = jnp.where(match == 1, seen[s][4], second_col)
        jobs[0] = jnp.where(count == 0, second_row, first_row)
        jobs[1] = jnp.where(count == 0, second_col, first_col)

    def masks(jobs, worker, place):
        wide = jnp.broadcast_to(jobs[1, pl.ds(worker, 1), :], (ROWS, W))
        tall = jnp.broadcast_to(jobs[0, pl.ds(worker, 1), :], (ROWS, W))
        return lane >= wide, place * ROWS + row >= tall

    def gather(it, k):
        jobs, bands_ref, place, targets = (
            (jobs_work, obj_work, member, members) if it else (jobs_own, obj, me, workers)
        )
        bands = [[[bands_ref[b, p, k, :, h * W : (h + 1) * W] for h in range(2)] for p in range(2)] for b in range(3)]
        for j in range(SCAN):
            left_part, before = masks(jobs, ring(place, j), place)
            for p in range(2):
                prev, own, after = [jnp.where(left_part, bands[b][p][0], bands[b][p][1]) for b in range(3)]
                merged = jnp.where(before, prev, after)
                if j == 0 and it:
                    patch[it, k, p, 0, rows_of(place), :] = merged
                    patch[it, k, p, 1, rows_of(place), :] = own
                else:
                    gather_out[it, k, j, p, 0] = merged
                    gather_out[it, k, j, p, 1] = own
            if j or not it:
                links.send(
                    "gather", (it, k, j), gather_out.at[it, k, j], patch.at[it, k, :, :, rows_of(place), :], targets[j],
                    None if j else same,
                )

    for j in range(1, SCAN):
        links.receive("meta_own", (j - 1,), meta_own.at[ring(me, -j)])
    assign(meta_own, jobs_own)
    local.pop("object").wait()
    for k in range(S):
        links.receive("near", (k, 0))
        links.receive("near", (k, 1))
        gather(0, k)
    links.send("replica", (0,), obj, obj_work, workers[0], same)

    for j in range(SCAN):
        links.receive("meta_work", (j,), meta_work.at[ring(member, -j)])
    assign(meta_work, jobs_work)
    my_row = jobs_work[0, pl.ds(member, 1), :]
    my_col = jobs_work[1, pl.ds(member, 1), :]
    for p in range(2):
        shift_probe[p] = shifted(shifted(probe[p], my_row, 0), my_col, 1)
    for name in ("lefts", "rights"):
        local.pop(name).wait()

    for it in range(ITERS):
        final = it == ITERS - 1

        def fetch(k):
            for j in range(1 if it else 0, SCAN):
                links.receive("gather", (it, k, j), patch.at[it, k, :, :, rows_of(ring(member, -j)), :])
            return patch[it, k, 0].reshape(W, W), patch[it, k, 1].reshape(W, W)

        def reduce_start(k, value):
            for p in range(2):
                grad[it, k, p] = value[p].reshape(2, W // 2, W)
            for j in range(0 if final else 1, SCAN):
                links.send(
                    "reduce", (it, k, j), grad.at[it, k, :, :, rows_of(ring(member, j)), :], grad_in.at[it, k, j],
                    region_owners[j] if final else members[j], None if j else same,
                )

        def reduce_end(k):
            jobs, place = (jobs_own, me) if final else (jobs_work, member)
            zero = jnp.zeros((ROWS, W), F32)
            total = [[[zero, zero] for p in range(2)] for b in range(3)]
            for j in range(SCAN):
                left_part, before = masks(jobs, ring(place, -j), place)
                if j or final:
                    links.receive("reduce", (it, k, j))
                for p in range(2):
                    if j or final:
                        merged, own = grad_in[it, k, j, p, 0], grad_in[it, k, j, p, 1]
                    else:
                        merged, own = grad[it, k, p, 0, rows_of(place), :], grad[it, k, p, 1, rows_of(place), :]
                    for b, term in ((0, jnp.where(before, merged, 0.0)), (1, own), (2, jnp.where(before, 0.0, merged))):
                        total[b][p][0] = total[b][p][0] + jnp.where(left_part, term, 0.0)
                        total[b][p][1] = total[b][p][1] + jnp.where(left_part, 0.0, term)
            for b in range(3):
                for p in range(2):
                    for h in range(2):
                        part[it, k, b, p, :, h * W : (h + 1) * W] = total[b][p][h]

        def pass_on(k):
            reduce_end(k)
            if final:
                for n, (d, b) in enumerate(LAST):
                    links.send("last", (k, n), part.at[it, k, b], last_in.at[k, n], near[d])
            else:
                for n, (d, b, w, at) in enumerate(CROSS):
                    links.send("cross", (k, n), part.at[it, k, pl.ds(b, w)], cross_in.at[k, pl.ds(at, w)], around[d])

        def update(k):
            if final:
                for n in range(len(LAST)):
                    links.receive("last", (k, n))
                for p in range(2):
                    gradient = part[it, k, 1, p] + last_in[k, 0, p] + last_in[k, 1, p]
                    out_ref[p, k] = out_base[p, k] - step * gradient
            else:
                for n in range(len(CROSS)):
                    links.receive("cross", (k, n))
                for b, (one, two) in enumerate(((0, 4), (1, 2), (3, 5))):
                    for p in range(2):
                        gradient = part[it, k, b, p] + cross_in[k, one, p] + cross_in[k, two, p]
                        obj_work[b, p, k] = obj_work[b, p, k] - step * gradient
                gather(it + 1, k)

        shone = (shift_probe[0], shift_probe[1])
        arrived = [shone]
        patches = [fetch(0)]
        wave = mul(shone, patches[0])
        for k in range(1, S):
            arrived.append(sandwich(*wave, left, right, PROP))
            patches.append(fetch(k))
            wave = mul(arrived[k], patches[k])
        far = sandwich(*wave, left, right, DFT)
        if it == 0:
            links.receive("meas", (0,))
            value = meas_in[0]
            for j in range(1, SCAN):
                links.receive("meas", (j,))
                take = jobs_work[pl.ds(2 + ring(member, -j), 1), pl.ds(member, 1), :].reshape(1, W)
                value = jnp.where(take == 1, meas_in[j], value)
            meas[...] = value
        ratio = meas[...] * lax.rsqrt(jnp.maximum(far[0] * far[0] + far[1] * far[1], 0.04))
        back = sandwich(far[0] - ratio * far[0], far[1] - ratio * far[1], left, right, DFT_C)
        for k in range(S - 1, 0, -1):
            reduce_start(k, mul_conj(arrived[k], back))
            back = sandwich(*mul_conj(patches[k], back), left, right, PROP_C)
        reduce_start(0, mul_conj(shone, back))

        pass_on(3)
        pass_on(2)
        links.receive("base" if final else "replica", (0,))
        update(3)
        pass_on(1)
        update(2)
        pass_on(0)
        update(1)
        update(0)
        if not final:
            links.send("base", (0,), obj_work.at[1], out_base, region_owners[0], same)

    links.finish()


def body(tiles, object_slices, probe_wave, offsets, counts, measured):
    lefts, rights = tables()
    dma = pltpu.SemaphoreType.DMA
    hbm = pl.BlockSpec(memory_space=pltpu.HBM)
    scratch = [
        pltpu.SMEM(offsets.shape, jnp.int32),
        pltpu.SMEM(counts.shape, jnp.int32),
        pltpu.VMEM((3, 2, S, ROWS, 2 * W), F32),
        pltpu.VMEM((3, 2, S, ROWS, 2 * W), F32),
        pltpu.VMEM((2, S, ROWS, 2 * W), F32),
        pltpu.VMEM((2, W, W), F32),
        pltpu.VMEM((2, W, W), F32),
        pltpu.VMEM((W, W), F32),
        pltpu.VMEM((SCAN, W, W), F32),
        pltpu.VMEM(lefts.shape, BF16),
        pltpu.VMEM(rights.shape, BF16),
        pltpu.VMEM((ROWS, W), jnp.int32),
        pltpu.VMEM((SCAN, ROWS, W), jnp.int32),
        pltpu.VMEM((SCAN, ROWS, W), jnp.int32),
        pltpu.VMEM((2 + SCAN, ROWS, W), jnp.int32),
        pltpu.VMEM((2 + SCAN, ROWS, W), jnp.int32),
        pltpu.VMEM((ITERS, S, 2, 2, W // 2, W), F32),
        pltpu.VMEM((ITERS, S, SCAN, 2, 2, ROWS, W), F32),
        pltpu.VMEM((ITERS, S, 2, 2, W // 2, W), F32),
        pltpu.VMEM((ITERS, S, SCAN, 2, 2, ROWS, W), F32),
        pltpu.VMEM((ITERS, S, 3, 2, ROWS, 2 * W), F32),
        pltpu.VMEM((S, 6, 2, ROWS, 2 * W), F32),
        pltpu.VMEM((S, 2, 2, ROWS, 2 * W), F32),
        dma((6,)),
    ]
    shapes = {
        "meta_own": (SCAN - 1,),
        "meta_work": (SCAN,),
        "near": (S, 2),
        "meas": (SCAN,),
        "replica": (1,),
        "gather": (ITERS, S, SCAN),
        "reduce": (ITERS, S, SCAN),
        "cross": (S, len(CROSS)),
        "base": (1,),
        "last": (S, len(LAST)),
    }
    for shape in shapes.values():
        scratch += [dma(shape), dma(shape)]
    return pl.pallas_call(
        functools.partial(kernel, tiles, tuple(shapes)),
        out_shape=jax.ShapeDtypeStruct(object_slices.shape, F32),
        in_specs=[hbm] * 7,
        out_specs=pl.BlockSpec(memory_space=pltpu.VMEM),
        scratch_shapes=scratch,
        compiler_params=pltpu.CompilerParams(
            collective_id=0, has_side_effects=True, vmem_limit_bytes=VMEM_BYTES
        ),
    )(offsets, counts, object_slices, probe_wave, measured, jnp.asarray(lefts), jnp.asarray(rights))


def solution(mesh):
    placed = (
        P(None, None, ("tile", "scan"), None),
        P(),
        P(("tile", "scan"), None),
        P(("tile", "scan")),
        P(("tile", "scan"), None, None),
    )
    return jax.shard_map(
        functools.partial(body, mesh.shape["tile"]),
        mesh=mesh,
        in_specs=placed,
        out_specs=P(None, None, ("tile", "scan"), None),
        check_vma=False,
    )
```

time: 78.9 us -> 72 us (0.913)
  the two profiles are of different devices: /device:TPU:105 before, /device:TPU:1 now
where the time goes in v2:
time: 72 us; the launch traced here: 71.9 us
  Pallas kernels  69.7 us (97%)
  local copies, waits for them, and re-layouts  1.47 us (2%)
    pallas_call x1, Pallas kernels, body(): pl.pallas_call(functools.partial(kernel, tiles, tuple(shapes)), out_shape...  69.7 us
    unnamed x1, local copies, waits for them, and re-layouts  1.47 us

profile of v2, /device:TPU:1, one launch (start us, length us, event | category | flops | bytes accessed | tf_op | source)
XLA Modules:
  0.0 71.9 jit_solution(17407293538365096096)
XLA Ops:
  0.7 69.7 %shard_map.73 = f32[2,4,8,256]{3,2,1,0:T(8,128)} custom-call(s32[2,2]{1,0:T(2,128)} %offsets_hbm.1, s32[1]{0:T(128)S(6)} %copy.9.counts_hbm, f32[2,4,8,256]{3,2,1,0:T(8,128)} %object_hbm.1, f32[2,128,128]{2,1,0:T(8,128)} %probe_hbm.1, f32[2,128,128]{2,1,0:T(8,128)} %measured_hbm.1, bf16[4,256,768]{2,1,0:T(8,128)(2,1)} %constant.4.clone.lefts_hbm, ...), custom_call_target="tpu_custom_call" | custom-call | tf_op jit(solution)/shard_map/pallas_call | solution.py:410
  70.4 1.5 %copy.10 = f32[2,4,8,256]{3,2,1,0:T(8,128)} copy(f32[2,4,8,256]{3,2,1,0:T(8,128)} %shard_map.73) | data formatting | bytes 131072

commit v3 on v2

--- a/solution.py
+++ b/solution.py
@@ -27,15 +27,30 @@
     dft = np.exp(-2j * np.pi * (n[:, None] * n[None, :] % W) / W) / np.sqrt(W)
     freq = (n + W // 2) % W - W // 2
     prop = np.conj(dft) @ (np.exp(-1j * np.pi * freq * freq / (2.0 * W))[:, None] * dft)
-    lefts, rights = [], []
-    for m in (prop, np.conj(prop), dft, np.conj(dft)):
-        right = np.block([[m.real, m.imag], [-m.imag, m.real]])
-        left = np.block([[m.real, -m.imag], [m.imag, m.real]])
-        for big, out, axis in ((right, rights, 0), (left, lefts, 1)):
-            high = big.astype(ml_dtypes.bfloat16)
-            low = (big - high.astype(np.float64)).astype(ml_dtypes.bfloat16)
-            out.append(np.concatenate([high, high, low], axis=axis))
-    return np.stack(lefts), np.stack(rights)
+    parts = []
+    for part in (prop.real, prop.imag, dft.real, dft.imag):
+        high = part.astype(ml_dtypes.bfloat16)
+        parts += [high, (part - high.astype(np.float64)).astype(ml_dtypes.bfloat16)]
+    return np.stack(parts)
+
+
+def spread(parts_ref, left_ref, right_ref):
+    for which, (first, sign) in enumerate(((0, 1), (0, -1), (4, 1), (4, -1))):
+        for place, low in enumerate((0, 0, 1)):
+            re = parts_ref[first + low]
+            im = parts_ref[first + 2 + low]
+            plus, minus = (im, -im) if sign == 1 else (-im, im)
+            at = low * 2 * W
+            if place:
+                left_ref[which, :W, at : at + W] = re
+                left_ref[which, :W, at + W : at + 2 * W] = minus
+                left_ref[which, W:, at : at + W] = plus
+                left_ref[which, W:, at + W : at + 2 * W] = re
+            at = place * 2 * W
+            right_ref[which, at : at + W, :W] = re
+            right_ref[which, at : at + W, W:] = plus
+            right_ref[which, at + W : at + 2 * W, :W] = minus
+            right_ref[which, at + W : at + 2 * W, W:] = re
 
 
 def halves(value):
@@ -45,9 +60,15 @@
 
 def sandwich(re, im, left_ref, right_ref, which):
     high, low = halves(jnp.concatenate([re, im], axis=0))
-    mid = jnp.dot(left_ref[which], jnp.concatenate([high, low, high], axis=0), preferred_element_type=F32)
+    left = left_ref[which]
+    both = jnp.dot(left[:, : 2 * W], jnp.concatenate([high, low], axis=1), preferred_element_type=F32)
+    mid = both[:, :W] + both[:, W:] + jnp.dot(left[:, 2 * W :], high, preferred_element_type=F32)
     high, low = halves(jnp.concatenate([mid[:W], mid[W:]], axis=1))
-    out = jnp.dot(jnp.concatenate([high, low, high], axis=1), right_ref[which], preferred_element_type=F32)
+    rows = jnp.concatenate([high, low, high], axis=1)
+    right = right_ref[which]
+    upper = jnp.dot(rows[: W // 2], right, preferred_element_type=F32)
+    lower = jnp.dot(rows[W // 2 :], right, preferred_element_type=F32)
+    out = jnp.concatenate([upper, lower], axis=0)
     return out[:, :W], out[:, W:]
 
 
@@ -71,18 +92,14 @@
         self.started = []
         self.open = {}
 
-    def send(self, name, index, src, dst, device, own=None):
+    def send(self, name, index, src, dst, device):
         send_sem, recv_sem = self.sems[name]
         copy = pltpu.make_async_remote_copy(
             src_ref=src, dst_ref=dst, send_sem=send_sem.at[index], recv_sem=recv_sem.at[index], device_id=device,
             device_id_type=MESH,
         )
-        if own is None:
-            copy.start()
-        else:
-            pl.when(own)(lambda: pltpu.make_async_copy(src, dst, recv_sem.at[index]).start())
-            pl.when(jnp.logical_not(own))(copy.start)
-        self.started.append((copy, own))
+        copy.start()
+        self.started.append(copy)
         self.open[name, index] = copy
 
     def receive(self, name, index, dst=None):
@@ -95,31 +112,23 @@
         copy.wait_recv()
 
     def finish(self):
-        for copy, own in self.started:
-            if own is None:
-                copy.wait_send()
-        if any(own is not None for _, own in self.started):
-            own = [own for _, own in self.started if own is not None][0]
-
-            @pl.when(jnp.logical_not(own))
-            def _():
-                for copy, own in self.started:
-                    if own is not None:
-                        copy.wait_send()
+        for copy in self.started:
+            copy.wait_send()
 
 
 CROSS = ((1, 1, 2, 0), (-1, 0, 2, 2), (2, 2, 1, 4), (-2, 0, 1, 5))
 LAST = ((1, 2), (-1, 0))
+BITS = (2, 1, 4)
 
 
 def twin(tile, scan):
-    core, half = lax.rem(tile, 2), lax.div(scan, 4)
-    return tile - core + half, lax.rem(scan, 4) + 4 * core
+    core, half, odd = lax.rem(tile, 2), lax.div(scan, 4), lax.rem(lax.div(tile, 2), 2)
+    return tile - core + half + 2 - 4 * odd, lax.rem(scan, 4) + 4 * core
 
 
 def kernel(
-    tiles, names, offsets_hbm, counts_hbm, object_hbm, probe_hbm, measured_hbm, lefts_hbm, rights_hbm, out_ref,
-    offsets_ref, counts_ref, obj, obj_work, out_base, probe, shift_probe, meas, meas_in, left, right, meta_out,
+    tiles, names, offsets_hbm, counts_hbm, object_hbm, probe_hbm, measured_hbm, parts_hbm, out_ref,
+    offsets_ref, counts_ref, obj, obj_work, out_base, probe, shift_probe, meas, meas_out, meas_in, parts, left, right, meta_out,
     meta_own, meta_work, jobs_own, jobs_work, patch, gather_out, grad, grad_in, part, cross_in, last_in, local_sem,
     *sems,
 ):
@@ -127,7 +136,6 @@
     tile = lax.axis_index("tile")
     me = lax.axis_index("scan")
     region, member = twin(tile, me)
-    same = region == tile
 
     def ring(first, j):
         return lax.rem(first + j + SCAN, SCAN)
@@ -136,20 +144,15 @@
     workers = [twin(tile, ring(me, j)) for j in range(SCAN)]
     members = [twin(region, ring(member, j)) for j in range(SCAN)]
     region_owners = [(region, ring(member, j)) for j in range(SCAN)]
+    partners = []
+    for bit in BITS:
+        upper = lax.rem(lax.div(member, bit), 2)
+        partners.append(twin(region, member + bit - 2 * bit * upper))
     near = {d: (lax.rem(tile + d + tiles, tiles), me) for d in (-1, 1)}
     around = {d: twin(lax.rem(region + d + tiles, tiles), member) for d in (-2, -1, 1, 2)}
 
     def rows_of(s):
         return pl.ds(pl.multiple_of(s * ROWS, ROWS), ROWS)
-
-    barrier = pltpu.get_barrier_semaphore()
-    others = owners[1:] + workers[1:] + members[1:] + region_owners[1:] + list(near.values()) + list(around.values())
-    for device in others:
-        pl.semaphore_signal(barrier, inc=1, device_id=device, device_id_type=MESH)
-
-    @pl.when(jnp.logical_not(same))
-    def _():
-        pl.semaphore_signal(barrier, inc=1, device_id=workers[0], device_id_type=MESH)
 
     local = {}
     for n, (name, src, dst) in enumerate(
@@ -158,12 +161,16 @@
             ("counts", counts_hbm, counts_ref),
             ("probe", probe_hbm, probe),
             ("object", object_hbm, obj.at[1]),
-            ("lefts", lefts_hbm, left),
-            ("rights", rights_hbm, right),
+            ("parts", parts_hbm, parts),
         )
     ):
         local[name] = pltpu.make_async_copy(src, dst, local_sem.at[n])
         local[name].start()
+
+    barrier = pltpu.get_barrier_semaphore()
+    others = owners[1:] + workers + members[1:] + region_owners + list(near.values()) + list(around.values())
+    for device in others:
+        pl.semaphore_signal(barrier, inc=1, device_id=device, device_id_type=MESH)
 
     row = lax.broadcasted_iota(jnp.int32, (ROWS, W), 0)
     lane = lax.broadcasted_iota(jnp.int32, (ROWS, W), 1)
@@ -176,43 +183,71 @@
     meta_out[...] = packed
     meta_own[me] = packed
 
-    pl.semaphore_wait(barrier, len(others) + jnp.where(same, 0, 1))
+    pl.semaphore_wait(barrier, len(others))
 
     for j in range(1, SCAN):
         links.send("meta_own", (j - 1,), meta_out, meta_own.at[me], owners[j])
     for j in range(SCAN):
-        links.send("meta_work", (j,), meta_out, meta_work.at[me], workers[j], None if j else same)
+        links.send("meta_work", (j,), meta_out, meta_work.at[me], workers[j])
     for k in range(S):
         links.send("near", (k, 0), object_hbm.at[:, k], obj.at[0, :, k], near[1])
         links.send("near", (k, 1), object_hbm.at[:, k], obj.at[2, :, k], near[-1])
-    links.send("meas", (0,), measured_hbm.at[0], meas_in.at[0], workers[0], same)
-    for j in range(1, SCAN):
-        links.send("meas", (j,), measured_hbm.at[1], meas_in.at[j], workers[j])
+    links.send("meas", (0,), measured_hbm, meas, workers[0])
     local.pop("probe").wait()
     intensity = probe[0] * probe[0] + probe[1] * probe[1]
     step = 0.5 / (jnp.max(intensity, keepdims=True) + 1e-06)
+    local.pop("parts").wait()
+    spread(parts, left, right)
+
+    def partner(value, bit):
+        upper = lax.rem(lax.div(row, bit), 2) == 1
+        if bit == SCAN // 2:
+            return pltpu.roll(value, bit, 0)
+        return jnp.where(upper, pltpu.roll(value, bit, 0), pltpu.roll(value, SCAN - bit, 0))
 
     def assign(meta, jobs):
-        seen = [[meta[s, f : f + 1, :] for f in range(5)] for s in range(SCAN)]
-        count = jnp.zeros((ROWS, W), jnp.int32)
-        first_row = first_col = second_row = second_col = empty_rank = count
-        empties = jnp.zeros((1, W), jnp.int32)
-        for s in range(SCAN):
-            here = row == s
-            count = jnp.where(here, seen[s][0], count)
-            first_row = jnp.where(here, seen[s][1], first_row)
-            first_col = jnp.where(here, seen[s][2], first_col)
-            empty_rank = jnp.where(here, empties, empty_rank)
-            empties = empties + jnp.where(seen[s][0] == 0, 1, 0)
-        doubles = jnp.zeros((1, W), jnp.int32)
-        for s in range(SCAN):
-            match = jnp.where((seen[s][0] == 2) & (doubles == empty_rank) & (count == 0), 1, 0)
-            doubles = doubles + jnp.where(seen[s][0] == 2, 1, 0)
-            jobs[2 + s] = match
-            second_row = jnp.where(match == 1, seen[s][3], second_row)
-            second_col = jnp.where(match == 1, seen[s][4], second_col)
-        jobs[0] = jnp.where(count == 0, second_row, first_row)
-        jobs[1] = jnp.where(count == 0, second_col, first_col)
+        fields = []
+        for f in range(5):
+            field = jnp.zeros((ROWS, W), jnp.int32)
+            for s in range(SCAN):
+                field = jnp.where(row == s, meta[s, f : f + 1, :], field)
+            fields.append(field)
+        count, lower, upper = fields[0], fields[1:3], fields[3:5]
+        for n, bit in enumerate(BITS):
+            rest = BITS[n + 1 :]
+            total = count
+            for other in rest:
+                total = total + partner(total, other)
+            excess = total - partner(total, bit)
+            eager = jnp.where(count > partner(count, bit), 1, 0)
+            rank = jnp.zeros((ROWS, W), jnp.int32)
+            ahead = eager
+            for other in rest:
+                rank = rank + jnp.where(lax.rem(lax.div(row, other), 2) == 1, partner(ahead, other), 0)
+                ahead = ahead + partner(ahead, other)
+            give = jnp.where((eager == 1) & (2 * rank < excess), 1, 0)
+            take = partner(give, bit)
+            jobs[2 + n] = count
+            jobs[5 + n] = take
+            for i in range(2):
+                handed = partner(jnp.where(count == 2, upper[i], lower[i]), bit)
+                lower[i] = jnp.where((take == 1) & (count == 0), handed, lower[i])
+                upper[i] = jnp.where((take == 1) & (count == 1), handed, upper[i])
+            count = count + take - give
+        jobs[0] = lower[0]
+        jobs[1] = lower[1]
+
+    def hand_over(n):
+        count = jobs_work[2 + n, pl.ds(member, 1), :]
+        meas_out[n] = jnp.where(count == 2, meas[1], meas[0])
+        links.send("hand", (n,), meas_out.at[n], meas_in.at[n], partners[n])
+
+    def take_over(n):
+        links.receive("hand", (n,))
+        count = jobs_work[2 + n, pl.ds(member, 1), :]
+        take = jobs_work[5 + n, pl.ds(member, 1), :]
+        for i in range(2):
+            meas[i] = jnp.where((take == 1) & (count == i), meas_in[n], meas[i])
 
     def masks(jobs, worker, place):
         wide = jnp.broadcast_to(jobs[1, pl.ds(worker, 1), :], (ROWS, W))
@@ -237,8 +272,7 @@
                     gather_out[it, k, j, p, 1] = own
             if j or not it:
                 links.send(
-                    "gather", (it, k, j), gather_out.at[it, k, j], patch.at[it, k, :, :, rows_of(place), :], targets[j],
-                    None if j else same,
+                    "gather", (it, k, j), gather_out.at[it, k, j], patch.at[it, k, :, :, rows_of(place), :], targets[j]
                 )
 
     for j in range(1, SCAN):
@@ -249,17 +283,20 @@
         links.receive("near", (k, 0))
         links.receive("near", (k, 1))
         gather(0, k)
-    links.send("replica", (0,), obj, obj_work, workers[0], same)
-
-    for j in range(SCAN):
-        links.receive("meta_work", (j,), meta_work.at[ring(member, -j)])
-    assign(meta_work, jobs_work)
+        if k == 0:
+            for j in range(SCAN):
+                links.receive("meta_work", (j,), meta_work.at[ring(member, -j)])
+            assign(meta_work, jobs_work)
+            links.receive("meas", (0,))
+            hand_over(0)
+
     my_row = jobs_work[0, pl.ds(member, 1), :]
     my_col = jobs_work[1, pl.ds(member, 1), :]
     for p in range(2):
         shift_probe[p] = shifted(shifted(probe[p], my_row, 0), my_col, 1)
-    for name in ("lefts", "rights"):
-        local.pop(name).wait()
+    take_over(0)
+    hand_over(1)
+    links.send("replica", (0,), obj, obj_work, workers[0])
 
     for it in range(ITERS):
         final = it == ITERS - 1
@@ -275,7 +312,7 @@
             for j in range(0 if final else 1, SCAN):
                 links.send(
                     "reduce", (it, k, j), grad.at[it, k, :, :, rows_of(ring(member, j)), :], grad_in.at[it, k, j],
-                    region_owners[j] if final else members[j], None if j else same,
+                    region_owners[j] if final else members[j],
                 )
 
         def reduce_end(k):
@@ -331,17 +368,14 @@
         for k in range(1, S):
             arrived.append(sandwich(*wave, left, right, PROP))
             patches.append(fetch(k))
+            if it == 0 and k == 1:
+                take_over(1)
+                hand_over(2)
             wave = mul(arrived[k], patches[k])
         far = sandwich(*wave, left, right, DFT)
         if it == 0:
-            links.receive("meas", (0,))
-            value = meas_in[0]
-            for j in range(1, SCAN):
-                links.receive("meas", (j,))
-                take = jobs_work[pl.ds(2 + ring(member, -j), 1), pl.ds(member, 1), :].reshape(1, W)
-                value = jnp.where(take == 1, meas_in[j], value)
-            meas[...] = value
-        ratio = meas[...] * lax.rsqrt(jnp.maximum(far[0] * far[0] + far[1] * far[1], 0.04))
+            take_over(2)
+        ratio = meas[0] * lax.rsqrt(jnp.maximum(far[0] * far[0] + far[1] * far[1], 0.04))
         back = sandwich(far[0] - ratio * far[0], far[1] - ratio * far[1], left, right, DFT_C)
         for k in range(S - 1, 0, -1):
             reduce_start(k, mul_conj(arrived[k], back))
@@ -350,21 +384,21 @@
 
         pass_on(3)
         pass_on(2)
+        pass_on(1)
         links.receive("base" if final else "replica", (0,))
         update(3)
-        pass_on(1)
+        pass_on(0)
         update(2)
-        pass_on(0)
         update(1)
         update(0)
         if not final:
-            links.send("base", (0,), obj_work.at[1], out_base, region_owners[0], same)
+            links.send("base", (0,), obj_work.at[1], out_base, region_owners[0])
 
     links.finish()
 
 
 def body(tiles, object_slices, probe_wave, offsets, counts, measured):
-    lefts, rights = tables()
+    parts = tables()
     dma = pltpu.SemaphoreType.DMA
     hbm = pl.BlockSpec(memory_space=pltpu.HBM)
     scratch = [
@@ -375,10 +409,12 @@
         pltpu.VMEM((2, S, ROWS, 2 * W), F32),
         pltpu.VMEM((2, W, W), F32),
         pltpu.VMEM((2, W, W), F32),
-        pltpu.VMEM((W, W), F32),
-        pltpu.VMEM((SCAN, W, W), F32),
-        pltpu.VMEM(lefts.shape, BF16),
-        pltpu.VMEM(rights.shape, BF16),
+        pltpu.VMEM((2, W, W), F32),
+        pltpu.VMEM((len(BITS), W, W), F32),
+        pltpu.VMEM((len(BITS), W, W), F32),
+        pltpu.VMEM(parts.shape, BF16),
+        pltpu.VMEM((4, 2 * W, 4 * W), BF16),
+        pltpu.VMEM((4, 6 * W, 2 * W), BF16),
         pltpu.VMEM((ROWS, W), jnp.int32),
         pltpu.VMEM((SCAN, ROWS, W), jnp.int32),
         pltpu.VMEM((SCAN, ROWS, W), jnp.int32),
@@ -391,13 +427,14 @@
         pltpu.VMEM((ITERS, S, 3, 2, ROWS, 2 * W), F32),
         pltpu.VMEM((S, 6, 2, ROWS, 2 * W), F32),
         pltpu.VMEM((S, 2, 2, ROWS, 2 * W), F32),
-        dma((6,)),
+        dma((5,)),
     ]
     shapes = {
         "meta_own": (SCAN - 1,),
         "meta_work": (SCAN,),
         "near": (S, 2),
-        "meas": (SCAN,),
+        "meas": (1,),
+        "hand": (len(BITS),),
         "replica": (1,),
         "gather": (ITERS, S, SCAN),
         "reduce": (ITERS, S, SCAN),
@@ -410,13 +447,13 @@
     return pl.pallas_call(
         functools.partial(kernel, tiles, tuple(shapes)),
         out_shape=jax.ShapeDtypeStruct(object_slices.shape, F32),
-        in_specs=[hbm] * 7,
+        in_specs=[hbm] * 6,
         out_specs=pl.BlockSpec(memory_space=pltpu.VMEM),
         scratch_shapes=scratch,
         compiler_params=pltpu.CompilerParams(
             collective_id=0, has_side_effects=True, vmem_limit_bytes=VMEM_BYTES
         ),
-    )(offsets, counts, object_slices, probe_wave, measured, jnp.asarray(lefts), jnp.asarray(rights))
+    )(offsets, counts, object_slices, probe_wave, measured, jnp.asarray(parts))
 
 
 def solution(mesh):

time: 72 us -> 68.5 us (0.951)
  Pallas kernels: 69.7 us -> 66.2 us
    pallas_call x1, Pallas kernels: 69.7 us -> 66.2 us  [body(): pl.pallas_call(functools.partial(kernel, tiles, tuple(shapes)), out_shape...]
where the time goes in v3:
time: 68.5 us; the launch traced here: 68.4 us
  Pallas kernels  66.2 us (97%)
  local copies, waits for them, and re-layouts  1.47 us (2%)
    pallas_call x1, Pallas kernels, body(): pl.pallas_call(functools.partial(kernel, tiles, tuple(shapes)), out_shape...  66.2 us
    unnamed x1, local copies, waits for them, and re-layouts  1.47 us

profile of v3, /device:TPU:1, one launch (start us, length us, event | category | flops | bytes accessed | tf_op | source)
XLA Modules:
  0.0 68.4 jit_solution(3456976119944253975)
XLA Ops:
  0.7 66.2 %shard_map.64 = f32[2,4,8,256]{3,2,1,0:T(8,128)} custom-call(s32[2,2]{1,0:T(2,128)} %offsets_hbm.1, s32[1]{0:T(128)S(6)} %copy.8.counts_hbm, f32[2,4,8,256]{3,2,1,0:T(8,128)} %object_hbm.1, f32[2,128,128]{2,1,0:T(8,128)} %probe_hbm.1, f32[2,128,128]{2,1,0:T(8,128)} %measured_hbm.1, bf16[8,128,128]{2,1,0:T(8,128)(2,1)} %constant.2.clone.parts_hbm), custom_call_target="tpu_custom_call" | custom-call | tf_op jit(solution)/shard_map/pallas_call | solution.py:447
  66.9 1.5 %copy.9 = f32[2,4,8,256]{3,2,1,0:T(8,128)} copy(f32[2,4,8,256]{3,2,1,0:T(8,128)} %shard_map.64) | data formatting | bytes 131072

commit v4 on v3

--- a/solution.py
+++ b/solution.py
@@ -14,6 +14,7 @@
 S = 4
 W = 128
 SCAN = 8
+FAR_FIRST = (2, 6, 1, 3, 5, 7, 4, 0)
 ROWS = 8
 PROP, PROP_C, DFT, DFT_C = range(4)
 MESH = pl.DeviceIdType.MESH
@@ -118,7 +119,7 @@
 
 CROSS = ((1, 1, 2, 0), (-1, 0, 2, 2), (2, 2, 1, 4), (-2, 0, 1, 5))
 LAST = ((1, 2), (-1, 0))
-BITS = (2, 1, 4)
+STAGES = ((4, 4, (1, 2)), (2, 3, (1,)), (1, 1, ()))
 
 
 def twin(tile, scan):
@@ -145,9 +146,12 @@
     members = [twin(region, ring(member, j)) for j in range(SCAN)]
     region_owners = [(region, ring(member, j)) for j in range(SCAN)]
     partners = []
-    for bit in BITS:
-        upper = lax.rem(lax.div(member, bit), 2)
-        partners.append(twin(region, member + bit - 2 * bit * upper))
+    for _, pair, _ in STAGES:
+        other = member
+        for bit in (1, 2, 4):
+            if pair % (2 * bit) // bit:
+                other = other + bit - 2 * bit * lax.rem(lax.div(member, bit), 2)
+        partners.append(twin(region, other))
     near = {d: (lax.rem(tile + d + tiles, tiles), me) for d in (-1, 1)}
     around = {d: twin(lax.rem(region + d + tiles, tiles), member) for d in (-2, -1, 1, 2)}
 
@@ -200,6 +204,8 @@
     spread(parts, left, right)
 
     def partner(value, bit):
+        if bit == 3:
+            return partner(partner(value, 1), 2)
         upper = lax.rem(lax.div(row, bit), 2) == 1
         if bit == SCAN // 2:
             return pltpu.roll(value, bit, 0)
@@ -213,24 +219,23 @@
                 field = jnp.where(row == s, meta[s, f : f + 1, :], field)
             fields.append(field)
         count, lower, upper = fields[0], fields[1:3], fields[3:5]
-        for n, bit in enumerate(BITS):
-            rest = BITS[n + 1 :]
+        for n, (bit, pair, rest) in enumerate(STAGES):
             total = count
             for other in rest:
                 total = total + partner(total, other)
             excess = total - partner(total, bit)
-            eager = jnp.where(count > partner(count, bit), 1, 0)
+            eager = jnp.where(count > partner(count, pair), 1, 0)
             rank = jnp.zeros((ROWS, W), jnp.int32)
             ahead = eager
             for other in rest:
                 rank = rank + jnp.where(lax.rem(lax.div(row, other), 2) == 1, partner(ahead, other), 0)
                 ahead = ahead + partner(ahead, other)
             give = jnp.where((eager == 1) & (2 * rank < excess), 1, 0)
-            take = partner(give, bit)
+            take = partner(give, pair)
             jobs[2 + n] = count
             jobs[5 + n] = take
             for i in range(2):
-                handed = partner(jnp.where(count == 2, upper[i], lower[i]), bit)
+                handed = partner(jnp.where(count == 2, upper[i], lower[i]), pair)
                 lower[i] = jnp.where((take == 1) & (count == 0), handed, lower[i])
                 upper[i] = jnp.where((take == 1) & (count == 1), handed, upper[i])
             count = count + take - give
@@ -259,7 +264,7 @@
             (jobs_work, obj_work, member, members) if it else (jobs_own, obj, me, workers)
         )
         bands = [[[bands_ref[b, p, k, :, h * W : (h + 1) * W] for h in range(2)] for p in range(2)] for b in range(3)]
-        for j in range(SCAN):
+        for j in FAR_FIRST:
             left_part, before = masks(jobs, ring(place, j), place)
             for p in range(2):
                 prev, own, after = [jnp.where(left_part, bands[b][p][0], bands[b][p][1]) for b in range(3)]
@@ -289,14 +294,16 @@
             assign(meta_work, jobs_work)
             links.receive("meas", (0,))
             hand_over(0)
-
+        if k == 1:
+            take_over(0)
+            hand_over(1)
+
+    take_over(1)
+    hand_over(2)
     my_row = jobs_work[0, pl.ds(member, 1), :]
     my_col = jobs_work[1, pl.ds(member, 1), :]
     for p in range(2):
         shift_probe[p] = shifted(shifted(probe[p], my_row, 0), my_col, 1)
-    take_over(0)
-    hand_over(1)
-    links.send("replica", (0,), obj, obj_work, workers[0])
 
     for it in range(ITERS):
         final = it == ITERS - 1
@@ -309,7 +316,7 @@
         def reduce_start(k, value):
             for p in range(2):
                 grad[it, k, p] = value[p].reshape(2, W // 2, W)
-            for j in range(0 if final else 1, SCAN):
+            for j in FAR_FIRST if final else FAR_FIRST[:-1]:
                 links.send(
                     "reduce", (it, k, j), grad.at[it, k, :, :, rows_of(ring(member, j)), :], grad_in.at[it, k, j],
                     region_owners[j] if final else members[j],
@@ -368,9 +375,8 @@
         for k in range(1, S):
             arrived.append(sandwich(*wave, left, right, PROP))
             patches.append(fetch(k))
-            if it == 0 and k == 1:
-                take_over(1)
-                hand_over(2)
+            if it == 0 and k == 2:
+                links.send("replica", (0,), obj, obj_work, workers[0])
             wave = mul(arrived[k], patches[k])
         far = sandwich(*wave, left, right, DFT)
         if it == 0:
@@ -382,12 +388,14 @@
             back = sandwich(*mul_conj(patches[k], back), left, right, PROP_C)
         reduce_start(0, mul_conj(shone, back))
 
-        pass_on(3)
-        pass_on(2)
-        pass_on(1)
+        for k in range(S - 1, 0, -1):
+            pass_on(k)
+        if not final:
+            pass_on(0)
         links.receive("base" if final else "replica", (0,))
         update(3)
-        pass_on(0)
+        if final:
+            pass_on(0)
         update(2)
         update(1)
         update(0)
@@ -410,8 +418,8 @@
         pltpu.VMEM((2, W, W), F32),
         pltpu.VMEM((2, W, W), F32),
         pltpu.VMEM((2, W, W), F32),
-        pltpu.VMEM((len(BITS), W, W), F32),
-        pltpu.VMEM((len(BITS), W, W), F32),
+        pltpu.VMEM((len(STAGES), W, W), F32),
+        pltpu.VMEM((len(STAGES), W, W), F32),
         pltpu.VMEM(parts.shape, BF16),
         pltpu.VMEM((4, 2 * W, 4 * W), BF16),
         pltpu.VMEM((4, 6 * W, 2 * W), BF16),
@@ -434,7 +442,7 @@
         "meta_work": (SCAN,),
         "near": (S, 2),
         "meas": (1,),
-        "hand": (len(BITS),),
+        "hand": (len(STAGES),),
         "replica": (1,),
         "gather": (ITERS, S, SCAN),
         "reduce": (ITERS, S, SCAN),

time: 68.5 us -> 67.5 us (0.985)
  Pallas kernels: 66.2 us -> 65.2 us
    pallas_call x1, Pallas kernels: 66.2 us -> 65.2 us  [body(): pl.pallas_call(functools.partial(kernel, tiles, tuple(shapes)), out_shape...]
where the time goes in v4:
time: 67.5 us; the launch traced here: 67.3 us
  Pallas kernels  65.2 us (97%)
  local copies, waits for them, and re-layouts  1.47 us (2%)
    pallas_call x1, Pallas kernels, body(): pl.pallas_call(functools.partial(kernel, tiles, tuple(shapes)), out_shape...  65.2 us
    unnamed x1, local copies, waits for them, and re-layouts  1.47 us

profile of v4, /device:TPU:1, one launch (start us, length us, event | category | flops | bytes accessed | tf_op | source)
XLA Modules:
  0.0 67.3 jit_solution(12950838992060389220)
XLA Ops:
  0.7 65.2 %shard_map.64 = f32[2,4,8,256]{3,2,1,0:T(8,128)} custom-call(s32[2,2]{1,0:T(2,128)} %offsets_hbm.1, s32[1]{0:T(128)S(6)} %copy.8.counts_hbm, f32[2,4,8,256]{3,2,1,0:T(8,128)} %object_hbm.1, f32[2,128,128]{2,1,0:T(8,128)} %probe_hbm.1, f32[2,128,128]{2,1,0:T(8,128)} %measured_hbm.1, bf16[8,128,128]{2,1,0:T(8,128)(2,1)} %constant.2.clone.parts_hbm), custom_call_target="tpu_custom_call" | custom-call | tf_op jit(solution)/shard_map/pallas_call | solution.py:455
  65.8 1.5 %copy.9 = f32[2,4,8,256]{3,2,1,0:T(8,128)} copy(f32[2,4,8,256]{3,2,1,0:T(8,128)} %shard_map.64) | data formatting | bytes 131072

commit v5 on v4

--- a/solution.py
+++ b/solution.py
@@ -189,11 +189,13 @@
 
     pl.semaphore_wait(barrier, len(others))
 
-    for j in range(1, SCAN):
+    for j in FAR_FIRST[:-1]:
         links.send("meta_own", (j - 1,), meta_out, meta_own.at[me], owners[j])
+    links.send("near", (0, 0), object_hbm.at[:, 0], obj.at[0, :, 0], near[1])
+    links.send("near", (0, 1), object_hbm.at[:, 0], obj.at[2, :, 0], near[-1])
     for j in range(SCAN):
         links.send("meta_work", (j,), meta_out, meta_work.at[me], workers[j])
-    for k in range(S):
+    for k in range(1, S):
         links.send("near", (k, 0), object_hbm.at[:, k], obj.at[0, :, k], near[1])
         links.send("near", (k, 1), object_hbm.at[:, k], obj.at[2, :, k], near[-1])
     links.send("meas", (0,), measured_hbm, meas, workers[0])

time: 67.5 us -> 67.4 us (level)
  no operation moved by 1% of the time
where the time goes in v5:
time: 67.4 us; the launch traced here: 67.2 us
  Pallas kernels  65.1 us (97%)
  local copies, waits for them, and re-layouts  1.47 us (2%)
    pallas_call x1, Pallas kernels, body(): pl.pallas_call(functools.partial(kernel, tiles, tuple(shapes)), out_shape...  65.1 us
    unnamed x1, local copies, waits for them, and re-layouts  1.47 us

profile of v5, /device:TPU:1, one launch (start us, length us, event | category | flops | bytes accessed | tf_op | source)
XLA Modules:
  0.0 67.2 jit_solution(10155218739433768498)
XLA Ops:
  0.7 65.1 %shard_map.64 = f32[2,4,8,256]{3,2,1,0:T(8,128)} custom-call(s32[2,2]{1,0:T(2,128)} %offsets_hbm.1, s32[1]{0:T(128)S(6)} %copy.8.counts_hbm, f32[2,4,8,256]{3,2,1,0:T(8,128)} %object_hbm.1, f32[2,128,128]{2,1,0:T(8,128)} %probe_hbm.1, f32[2,128,128]{2,1,0:T(8,128)} %measured_hbm.1, bf16[8,128,128]{2,1,0:T(8,128)(2,1)} %constant.2.clone.parts_hbm), custom_call_target="tpu_custom_call" | custom-call | tf_op jit(solution)/shard_map/pallas_call | solution.py:457
  65.7 1.5 %copy.9 = f32[2,4,8,256]{3,2,1,0:T(8,128)} copy(f32[2,4,8,256]{3,2,1,0:T(8,128)} %shard_map.64) | data formatting | bytes 131072
